TPU v7x, 32 devices: a whole 2x2x4 slice. The times are simulated.
32 devices in a mesh: grp: 2 (over y), rec: 4 (over z), chan: 2 (over x), fft: 2 (over core).
Axes of the slice: x: 2, y: 2, z: 4, core: 2. Of those that a mesh axis runs over, the one named last changes fastest.
Arguments:
- record_ids: int32 [8], P(('grp', 'rec')), parts along dimension 0, may hold values from 0 to 63
- rotations: float32 [64, 3, 3], replicated, as said below
- ligand_coords: int32 [3, 1024], P(None, 'grp'), parts along dimension 1, may hold values from -4096 to 4096
- atom_types: int32 [1024], P('grp'), parts along dimension 0, may hold values from 0 to 17
- channel_weights: float32 [18, 2], P(None, 'chan'), may hold values from -6 to 6
- receptor_spectra: float32 [4, 2, 2, 64, 4096], P('rec', 'chan', None, None, 'fft'), may hold values from -24 to 24
Outputs:
- energy: float32 [8, 64, 4096], P(('grp', 'rec'), 'fft', 'chan'), parts along dimension 0
There are 2 independent parts, one for each index of `grp`. A program takes and returns all parts, laid end to end along the dimension named above; an argument that names none is the same for every part. Nothing has to cross between parts.
Inputs may be any that keep to these rules, and one draw needn't show every extreme that they name: `rotations`: each [3, 3] block is a rotation matrix: orthonormal with determinant 1.
All inputs are finite; a program needn't handle non-finite values.
Results may differ from a plain program's by a relative error of at most 0.0003.
Values sent between devices are 32-bit elements; how exact they have to be, the bound alone decides.
A program may use at most 64 MiB of HBM per device.

v0:
```python
import math

import jax
import jax.numpy as jnp
from jax import lax
from jax.sharding import PartitionSpec as P

GRID = 64


HIGHEST = lax.Precision.HIGHEST


def from_behind(value, axis, steps):
    count = lax.axis_size(axis)
    pairs = [(source, (source + steps) % count) for source in range(count)]
    return lax.ppermute(value, axis, pairs)


def dft_tables(count):
    index = jnp.arange(count, dtype=jnp.int32)
    phase = index[:, None] * index[None, :] % count
    angle = phase.astype(jnp.float32) * (2.0 * math.pi / count)
    return (jnp.cos(angle), jnp.sin(angle))


def hat_rows(places, cells):
    return jnp.maximum(0.0, 1.0 - jnp.abs(places[:, None] - cells[None, :]))


def correlate(ligand, receptor):
    ligand_real = ligand[:, :, 0]
    ligand_imaginary = ligand[:, :, 1]
    receptor_real = receptor[None, :, 0]
    receptor_imaginary = receptor[None, :, 1]
    real_part = ligand_real * receptor_real + ligand_imaginary * receptor_imaginary
    imaginary_part = ligand_real * receptor_imaginary - ligand_imaginary * receptor_real
    return jnp.stack([real_part, imaginary_part], axis=2)


def rows_forward(spectrum, cosine, sine):
    real_part = spectrum[:, :, 0]
    imaginary_part = spectrum[:, :, 1]
    real_out = jnp.einsum("kx,rcxm->rckm", cosine, real_part, precision=HIGHEST) + jnp.einsum(
        "kx,rcxm->rckm", sine, imaginary_part, precision=HIGHEST
    )
    imaginary_out = jnp.einsum(
        "kx,rcxm->rckm", cosine, imaginary_part, precision=HIGHEST
    ) - jnp.einsum("kx,rcxm->rckm", sine, real_part, precision=HIGHEST)
    return jnp.stack([real_out, imaginary_out], axis=2)


def rows_inverse(spectrum, cosine, sine):
    real_part = spectrum[:, :, 0]
    imaginary_part = spectrum[:, :, 1]
    real_out = jnp.einsum("xk,rckm->rcxm", cosine, real_part, precision=HIGHEST) - jnp.einsum(
        "xk,rckm->rcxm", sine, imaginary_part, precision=HIGHEST
    )
    imaginary_out = jnp.einsum(
        "xk,rckm->rcxm", cosine, imaginary_part, precision=HIGHEST
    ) + jnp.einsum("xk,rckm->rcxm", sine, real_part, precision=HIGHEST)
    return jnp.stack([real_out, imaginary_out], axis=2)


def energies(total, cosine, sine):
    records = total.shape[0]
    channels = total.shape[1]
    turned = rows_inverse(total, cosine, sine)
    halves = lax.all_to_all(turned, "fft", split_axis=3, concat_axis=4, tiled=True)
    slab = halves.shape[3]
    volume = halves.reshape(records, channels, 2, slab, GRID, GRID)
    real_part = volume[:, :, 0]
    imaginary_part = volume[:, :, 1]
    real_y = jnp.einsum("yk,rcxkz->rcxyz", cosine, real_part, precision=HIGHEST) - jnp.einsum(
        "yk,rcxkz->rcxyz", sine, imaginary_part, precision=HIGHEST
    )
    imaginary_y = jnp.einsum(
        "yk,rcxkz->rcxyz", cosine, imaginary_part, precision=HIGHEST
    ) + jnp.einsum("yk,rcxkz->rcxyz", sine, real_part, precision=HIGHEST)
    scores = jnp.einsum("rcxyk,zk->rcxyz", real_y, cosine, precision=HIGHEST) - jnp.einsum(
        "rcxyk,zk->rcxyz", imaginary_y, sine, precision=HIGHEST
    )
    scores = scores * (1.0 / float(GRID**3))
    summed = jnp.sum(scores, axis=1).reshape(records, slab, GRID * GRID)
    return lax.psum_scatter(summed, "chan", scatter_dimension=2, tiled=True)


def finish(total, cosine, sine):
    return energies(total, cosine, sine)


def body(record_ids, rotations, ligand_coords, atom_types, channel_weights, receptor_spectra):
    parts = lax.axis_size("fft")
    slab = GRID // parts
    records = record_ids.shape[0]
    channels = channel_weights.shape[1]
    width = GRID * GRID
    cosine, sine = dft_tables(GRID)
    table_rows = rotations.shape[0]
    picks = (record_ids[:, None] == jnp.arange(table_rows, dtype=jnp.int32)[None, :]).astype(
        jnp.float32
    )
    chosen = jnp.dot(picks, rotations.reshape(table_rows, 9), precision=HIGHEST)
    kinds = channel_weights.shape[0]
    type_hot = (atom_types[:, None] == jnp.arange(kinds, dtype=jnp.int32)[None, :]).astype(
        jnp.float32
    )
    atom_weights = jnp.dot(type_hot, channel_weights, precision=HIGHEST)
    coords = ligand_coords.astype(jnp.float32) * (1.0 / 256.0)
    cells = jnp.arange(GRID, dtype=jnp.float32)
    slab_cells = (lax.axis_index("fft") * slab).astype(jnp.float32) + jnp.arange(
        slab, dtype=jnp.float32
    )

    def grid_record(matrix):
        places = [
            0.5 * GRID
            + (
                matrix[3 * axis_row] * coords[0]
                + matrix[3 * axis_row + 1] * coords[1]
                + matrix[3 * axis_row + 2] * coords[2]
            )
            for axis_row in range(3)
        ]
        row_hats = hat_rows(places[0], slab_cells)
        column_hats = hat_rows(places[1], cells)
        depth_hats = hat_rows(places[2], cells)
        weighted = atom_weights.T[:, None, :] * row_hats.T[None, :, :]
        spread = weighted[:, :, None, :] * column_hats.T[None, None, :, :]
        return jnp.einsum("cxya,az->cxyz", spread, depth_hats, precision=HIGHEST).reshape(
            channels, slab, width
        )

    grids = lax.map(grid_record, chosen)
    volume = grids.reshape(records, channels, slab, GRID, GRID)
    real_z = jnp.einsum("rcxyz,zk->rcxyk", volume, cosine, precision=HIGHEST)
    imaginary_z = -jnp.einsum("rcxyz,zk->rcxyk", volume, sine, precision=HIGHEST)
    real_y = jnp.einsum("ky,rcxyz->rcxkz", cosine, real_z, precision=HIGHEST) + jnp.einsum(
        "ky,rcxyz->rcxkz", sine, imaginary_z, precision=HIGHEST
    )
    imaginary_y = jnp.einsum(
        "ky,rcxyz->rcxkz", cosine, imaginary_z, precision=HIGHEST
    ) - jnp.einsum("ky,rcxyz->rcxkz", sine, real_z, precision=HIGHEST)
    halves = jnp.stack([real_y, imaginary_y], axis=2).reshape(records, channels, 2, slab, width)
    columns = lax.all_to_all(halves, "fft", split_axis=4, concat_axis=3, tiled=True)
    ligand = rows_forward(columns, cosine, sine)
    own_sum = jnp.sum(receptor_spectra, axis=0)
    total = correlate(ligand, own_sum)
    travelling = jnp.stack([ligand, total])
    for step in range(2):
        moved = from_behind(travelling, "rec", 1)
        travelling = moved.at[1].add(correlate(moved[0], own_sum))
    result = finish(travelling[1], cosine, sine)
    return result


def solution(mesh):
    in_specs = (
        P(("grp", "rec")),
        P(),
        P(None, "grp"),
        P("grp"),
        P(None, "chan"),
        P("rec", "chan", None, None, "fft"),
    )
    out_specs = P(("grp", "rec"), "fft", "chan")
    return jax.shard_map(body, mesh=mesh, in_specs=in_specs, out_specs=out_specs, check_vma=False)
```

profile of v0, /device:TPU:0, one launch (start us, length us, event | category | flops | bytes accessed | tf_op | source)
XLA Modules:
  0.0 226.0 jit_solution(10962600625535590408)
XLA Ops:
  6.5 0.7 reshape.405
  7.9 0.1 convolution_bitcast_fusion
  8.0 0.7 fusion.164
  8.7 0.7 convert_multiply_fusion
  9.4 5.7 %add_add_fusion = (f32[1,512]{1,0:T(1,128)S(1)}, f32[1,512]{1,0:T(1,128)S(1)}, f32[1,512]{1,0:T(1,128)S(1)}) fusion(f32[]{:T(128)} %bitcast.16, f32[]{:T(128)} %bitcast.15, f32[]{:T(128)} %bitcast.14, f32[3,512]{1,0:T(4,128)S(1)} %convert_multiply_fusion, f32[]{:T(128)} %bitcast.8, f32[]{:T(128)} %bitcast.7, f32[]{:T(128)} %bitcast.6, f32[]{:T(128)} %bitcast.12, ...), kind=kLoop, calls=%fused_computation.106 | loop fusion | flops 9216 | bytes 12324 | tf_op jit(solution)/shard_map/while/body/eval_jaxpr/add | solution.py:117
  15.1 1.0 fusion.23
  16.1 0.1 maximum_multiply_fusion
  16.2 3.5 %fusion = f32[32,64,64]{2,1,0:T(8,128)S(1)} fusion(f32[64,512]{1,0:T(8,128)S(1)} %subtract_maximum_fusion, f32[32,512]{1,0:T(8,128)S(1)} %maximum_multiply_fusion, f32[512]{0:T(512)S(1)} %bitcast.233), kind=kOutput, calls=%fused_computation | convolution fusion | flops 806486016 | bytes 722944 | tf_op jit(solution)/shard_map/while/body/eval_jaxpr/cxya,az->cxyz/dot_general | solution.py:130
  19.7 3.2 %fusion.51 = f32[32,64,64]{1,2,0:T(8,128)S(1)} fusion(f32[32,64,64]{2,1,0:T(8,128)S(1)} %fusion), kind=kOutput, calls=%fused_computation.98 | convolution fusion | flops 100720640 | bytes 1048576 | tf_op jit(solution)/shard_map/rcxyz,zk->rcxyk/dot_general | solution.py:136
  23.0 1.1 convolution_negate_fusion
  24.1 1.1 fusion.49
  25.2 1.8 fusion.47
  27.0 1.8 fusion.10
  28.9 1.3 copy.40
  30.2 2.6 %stack.63 = f32[1,1,1,32,4096]{4,3,2,1,0:T(8,128)} reshape(f32[1,1,32,64,64]{4,3,2,1,0:T(8,128)} %copy.40) | data formatting | bytes 1048576 | tf_op jit(solution)/shard_map/stack | solution.py:144
  32.8 1.1 fusion.9
  34.0 0.3 copy.43
  34.3 0.4 stack.64
  34.7 0.3 copy-done.2
  35.0 0.1 pad_maximum_fusion.1
  35.1 4.4 %copy.44 = f32[1,1,2,32,4096]{3,2,1,0,4:T(2,128)} copy(f32[1,1,2,32,4096]{4,3,2,1,0:T(8,128)S(1)} %pad_maximum_fusion.1) | data formatting | bytes 2097152 | tf_op jit(solution)/shard_map/stack | solution.py:144
  39.5 5.7 %reshape.425 = f32[2,1,131072]{2,1,0:T(1,128)S(1)} reshape(f32[4096,1,1,2,32]{4,3,2,1,0:T(2,128)} %bitcast.217) | data formatting | bytes 2097152
  45.2 4.6 %all_to_all.33 = f32[2,1,131072]{2,1,0:T(1,128)S(1)} all-to-all(f32[2,1,131072]{2,1,0:T(1,128)S(1)} %reshape.425), channel_id=1, replica_groups=mesh['grp'=2,'rec'=4,'chan'=2,'fft'=2] {'fft'}, dimensions={0} | all-to-all | bytes 2097152 | tf_op jit(solution)/shard_map/all_to_all | solution.py:145
  49.7 0.5 broadcast.311
  50.3 4.0 %reduce.4 = f32[2,131072]{1,0:T(2,128)S(1)} reduce(f32[2,1,131072]{2,1,0:T(1,128)S(1)} %all_to_all.33, f32[]{:T(128)} %broadcast.311), dimensions={1}, to_apply=%all_to_all.24.reduce_sub_computation | reduce | bytes 2097156 | tf_op jit(solution)/shard_map/all_to_all | solution.py:145
  54.3 5.8 %reshape.426 = f32[4096,1,1,2,32]{4,3,2,1,0:T(2,128)} reshape(f32[2,131072]{1,0:T(2,128)S(1)} %reduce.4) | data formatting | bytes 2097152
  60.1 5.3 %copy.58 = f32[1,1,2,32,2,2048]{5,4,3,2,1,0:T(2,128)S(1)} copy(f32[1,1,2,32,2,2048]{3,2,5,4,1,0:T(2,128)} %bitcast.218) | data formatting | bytes 2097152 | tf_op jit(solution)/shard_map/all_to_all | solution.py:145
  65.4 0.6 copy.46
  66.1 0.7 fusion.19
  66.8 0.0 copy-start.1
  66.8 0.7 fusion.20
  67.6 0.7 convolution_add_fusion.1
  68.3 0.7 convolution_subtract_fusion.1
  69.1 0.1 fusion.18
  69.2 0.2 maximum_bitcast_fusion
  69.5 0.2 pad_maximum_fusion
  69.7 16.0 %collective-permute-start = (f32[2,1,1,2,64,2048]{5,4,3,2,1,0:T(8,128)S(1)}, f32[2,1,1,2,64,2048]{5,4,3,2,1,0:T(8,128)S(1)}, u32[]{:S(2)}, u32[]{:S(2)}) collective-permute-start(f32[2,1,1,2,64,2048]{5,4,3,2,1,0:T(8,128)S(1)} %pad_maximum_fusion), channel_id=1, source_target_pairs={{0,4},{4,8},{8,12},{12,0},{1,5},{5,9},{9,13},{13,1},{2,6},{6,10},{... | collective-permute-start | bytes 6291464 | tf_op jit(solution)/shard_map/ppermute | solution.py:17
  85.7 48.0 %collective-permute-done = f32[2,1,1,2,64,2048]{5,4,3,2,1,0:T(8,128)S(1)} collective-permute-done((f32[2,1,1,2,64,2048]{5,4,3,2,1,0:T(8,128)S(1)}, f32[2,1,1,2,64,2048]{5,4,3,2,1,0:T(8,128)S(1)}, u32[]{:S(2)}, u32[]{:S(2)}) %collective-permute-start) | collective-permute-done | bytes 2097184 | tf_op jit(solution)/shard_map/ppermute | solution.py:17
  133.7 0.1 slice_bitcast_fusion.3
  133.8 0.2 add_bitcast_fusion.1
  133.9 0.3 fusion.12
  134.2 0.1 collective-permute-start.1
  134.3 48.9 %collective-permute-done.1 = f32[2,1,1,2,64,2048]{5,4,3,2,1,0:T(8,128)S(1)} collective-permute-done((f32[2,1,1,2,64,2048]{5,4,3,2,1,0:T(8,128)S(1)}, f32[2,1,1,2,64,2048]{5,4,3,2,1,0:T(8,128)S(1)}, u32[]{:S(2)}, u32[]{:S(2)}) %collective-permute-start.1) | collective-permute-done | bytes 2097184 | tf_op jit(solution)/shard_map/ppermute | solution.py:17
  183.2 0.1 slice_bitcast_fusion.2
  183.3 0.2 add_bitcast_fusion
  183.5 0.1 fusion.11
  183.6 0.7 fusion.21
  184.4 0.7 fusion.22
  185.1 0.7 fusion.2
  185.9 0.7 fusion.3
  186.6 0.1 pad_maximum_fusion.2
  186.7 0.8 copy.47
  187.5 4.6 %all_to_all.34 = f32[1,1,2,64,2048]{4,2,1,0,3:T(2,128)S(1)} all-to-all(f32[1,1,2,64,2048]{4,2,1,0,3:T(2,128)S(1)} %copy.47), channel_id=1, replica_groups=mesh['grp'=2,'rec'=4,'chan'=2,'fft'=2] {'fft'}, dimensions={3} | all-to-all | bytes 2097152 | tf_op jit(solution)/shard_map/all_to_all | solution.py:69
  192.1 0.8 copy.62
  192.9 1.2 reshape.412
  194.1 1.8 fusion.14
  195.9 1.8 fusion.13
  197.8 1.8 fusion.7
  199.6 1.8 fusion.8
  201.4 1.8 fusion.44
  203.3 1.8 fusion.6
  205.1 1.2 reshape.417
  206.3 0.0 reduce-scatter.2.cloned.1.call-update
  206.3 12.7 %reduce-scatter.2.cloned.1.call-done = f32[1,32,2048]{2,1,0:T(8,128)} async-done(((f32[1,32,4096]{2,1,0:T(8,128)}), f32[1,32,2048]{2,1,0:T(8,128)}) %reduce-scatter.2.cloned.1.call-update) | async-done | bytes 262160 | tf_op jit(solution)/shard_map/reduce_scatter | solution.py:85
  (7 shorter events, 0.0 us)
Async XLA Ops:
  6.5 8.6 %copy-start = (f32[18,1]{0,1:T(1,128)S(1)}, f32[18,1]{0,1:T(1,128)}, u32[]{:S(2)}) copy-start(f32[18,1]{0,1:T(1,128)} %param.14) | copy-start | bytes 220
  6.5 212.4 %reduce-scatter.2.cloned.1.call-start = ((), (), s32[]{:S(2)}) async-start(), calls=%async_computation.3 | async-start | bytes 786432 | tf_op jit(solution)/shard_map/reduce_scatter | solution.py:85
  33.9 1.0 copy-start.2
  66.8 2.3 %copy-start.1 = (f32[1,1,2,64,2048]{4,3,2,1,0:T(8,128)S(1)}, f32[1,1,2,64,2048]{4,3,2,1,0:T(8,128)}, u32[]{:S(2)}) copy-start(f32[1,1,2,64,2048]{4,3,2,1,0:T(8,128)} %param.15) | copy-start | bytes 3145732
  69.7 64.0 %collective-permute-start = (f32[2,1,1,2,64,2048]{5,4,3,2,1,0:T(8,128)S(1)}, f32[2,1,1,2,64,2048]{5,4,3,2,1,0:T(8,128)S(1)}, u32[]{:S(2)}, u32[]{:S(2)}) collective-permute-start(f32[2,1,1,2,64,2048]{5,4,3,2,1,0:T(8,128)S(1)} %pad_maximum_fusion), channel_id=1, source_target_pairs={{0,4},{4,8},{8,12},{12,0},{1,5},{5,9},{9,13},{13,1},{2,6},{6,10},{... | collective-permute-start | bytes 6291464 | tf_op jit(solution)/shard_map/ppermute | solution.py:17
  134.2 49.0 %collective-permute-start.1 = (f32[2,1,1,2,64,2048]{5,4,3,2,1,0:T(8,128)S(1)}, f32[2,1,1,2,64,2048]{5,4,3,2,1,0:T(8,128)S(1)}, u32[]{:S(2)}, u32[]{:S(2)}) collective-permute-start(f32[2,1,1,2,64,2048]{5,4,3,2,1,0:T(8,128)S(1)} %fusion.12), channel_id=1, source_target_pairs={{0,4},{4,8},{8,12},{12,0},{1,5},{5,9},{9,13},{13,1},{2,6},{6,10},{... | collective-permute-start | bytes 6291464 | tf_op jit(solution)/shard_map/ppermute | solution.py:17
Sparse Core Ops, SparseCore 0:
  206.4 12.5 reduce-scatter.1
where the time goes:
time: 229 us; the launch traced here: 226 us
  waiting for transfers between devices  110 us (48%)
  local copies, waits for them, and re-layouts  32.9 us (14%)
  matrix products  31.7 us (14%)
  starting transfers between devices  16.1 us (7%)
  between operations  14.6 us (6%)
  other arithmetic  12 us (5%)
  blocking collectives  9.15 us (4%)
    ppermute x2, waiting for transfers between devices, from_behind(): return lax.ppermute(value, axis, pairs)  96.9 us
    ppermute x2, starting transfers between devices, from_behind(): return lax.ppermute(value, axis, pairs)  16.1 us
    reduce_scatter x1, waiting for transfers between devices, energies(): return lax.psum_scatter(summed, 'chan', scatter_dimension=2, tiled=True)  12.7 us
    unnamed x8, local copies, waits for them, and re-layouts  11.9 us
    another operation x3, local copies, waits for them, and re-layouts, body(): jnp.stack([real_y, imaginary_y], axis=2)  7.4 us
    all_to_all x3, local copies, waits for them, and re-layouts, body(): lax.all_to_all(halves, 'fft', split_axis=4, concat_axis=3, tiled=True)  6.45 us
    add x1, other arithmetic, grid_record(): 0.5 * GRID  5.66 us
  transfers between devices with their start and end apart: 3, of which 3 were waited for; matrix products, arithmetic and copies ran while one was open for 0% of the time, Pallas kernels for 0%

commit v1 on v0

v1 whole, which is shorter than its diff:
```python
import math

import jax
import jax.numpy as jnp
from jax import lax
from jax.sharding import PartitionSpec as P

GRID = 64
HALF = GRID // 2
HIGHEST = lax.Precision.HIGHEST
HIGH = lax.Precision.HIGH


def from_behind(value, axis, steps):
    count = lax.axis_size(axis)
    pairs = [(source, (source + steps) % count) for source in range(count)]
    return lax.ppermute(value, axis, pairs)


def waves(rows, columns):
    phase = rows[:, None] * columns[None, :] % GRID
    angle = phase.astype(jnp.float32) * (2.0 * math.pi / GRID)
    return jnp.cos(angle), jnp.sin(angle)


def hat_rows(places, cells):
    return jnp.maximum(0.0, 1.0 - jnp.abs(places[:, None] - cells[None, :]))


def fold(receptor, width):
    lane = jnp.arange(width, dtype=jnp.int32)
    upper = receptor[:, HALF:]
    other = lax.ppermute(upper, "fft", [(0, 1), (1, 0)])
    source = jnp.where(lane < GRID, upper, other)
    back = lax.rev(source, (1, 2))
    mirrored = jnp.where(lane % GRID == 0, jnp.roll(back, 1, axis=2), jnp.roll(back, 65, axis=2))
    sign = jnp.array([1.0, -1.0], jnp.float32)[:, None, None]
    inner = mirrored[:, : HALF - 1] * sign
    inner = jnp.pad(inner, ((0, 0), (1, 1), (0, 0)))
    return receptor[:, : HALF + 1] + inner


def ligand_spectrum(record, rotations, ligand_coords, atom_types, channel_weights, width):
    table_rows = rotations.shape[0]
    picks = (record[:, None] == jnp.arange(table_rows, dtype=jnp.int32)[None, :]).astype(
        jnp.float32
    )
    matrix = jnp.dot(picks, rotations.reshape(table_rows, 9), precision=HIGHEST)[0]
    kinds = channel_weights.shape[0]
    type_hot = (atom_types[:, None] == jnp.arange(kinds, dtype=jnp.int32)[None, :]).astype(
        jnp.float32
    )
    weights = jnp.dot(type_hot, channel_weights, precision=HIGHEST)
    coords = ligand_coords.astype(jnp.float32) * (1.0 / 256.0)
    cells = jnp.arange(GRID, dtype=jnp.float32)
    hats = []
    for row in range(3):
        places = 0.5 * GRID + (
            matrix[3 * row] * coords[0]
            + matrix[3 * row + 1] * coords[1]
            + matrix[3 * row + 2] * coords[2]
        )
        hats.append(hat_rows(places, cells))
    index = jnp.arange(GRID, dtype=jnp.int32)
    lane = jnp.arange(width, dtype=jnp.int32)
    ky = lane // GRID + lax.axis_index("fft") * (width // GRID)
    y_cos, y_sin = waves(index, ky)
    z_cos, z_sin = waves(index, lane % GRID)
    x_cos, x_sin = waves(index, jnp.arange(HALF + 1, dtype=jnp.int32))
    y_hat = hats[1] * weights
    y_re = jnp.dot(y_hat, y_cos, precision=HIGH)
    y_im = jnp.dot(y_hat, y_sin, precision=HIGH)
    z_re = jnp.dot(hats[2], z_cos, precision=HIGH)
    z_im = jnp.dot(hats[2], z_sin, precision=HIGH)
    v_re = y_re * z_re - y_im * z_im
    v_im = y_re * z_im + y_im * z_re
    x_re = jnp.einsum("ax,xk->ka", hats[0], x_cos, precision=HIGH)
    x_im = jnp.einsum("ax,xk->ka", hats[0], x_sin, precision=HIGH)
    real = jnp.dot(x_re, v_re, precision=HIGH) - jnp.dot(x_im, v_im, precision=HIGH)
    imaginary = jnp.dot(x_re, v_im, precision=HIGH) + jnp.dot(x_im, v_re, precision=HIGH)
    return real, imaginary


def body(record_ids, rotations, ligand_coords, atom_types, channel_weights, receptor_spectra):
    width = receptor_spectra.shape[-1]
    slab = GRID // lax.axis_size("fft")
    record = from_behind(record_ids, "rec", 2)
    folded = fold(receptor_spectra[0, 0], width)
    pair = folded + from_behind(folded, "rec", 1)
    window = folded + from_behind(pair, "rec", 1)
    lig_re, lig_im = ligand_spectrum(
        record, rotations, ligand_coords, atom_types, channel_weights, width
    )
    product_re = lig_re * window[0] - lig_im * window[1]
    product_im = lig_re * window[1] + lig_im * window[0]
    index = jnp.arange(GRID, dtype=jnp.int32)
    cosine, sine = waves(index, jnp.arange(HALF + 1, dtype=jnp.int32))
    product = jnp.concatenate([product_re, product_im], axis=0)
    scale = 1.0 / float(GRID**3)
    turn = (
        jnp.concatenate(
            [
                jnp.concatenate([cosine, -sine], axis=1),
                jnp.concatenate([sine, cosine], axis=1),
            ],
            axis=0,
        )
        * scale
    )
    turned = jnp.dot(turn, product, precision=HIGH).reshape(1, 2, GRID, width)
    halves = lax.all_to_all(turned, "fft", split_axis=2, concat_axis=3, tiled=True)
    volume = halves.reshape(2, slab, GRID, GRID)
    cosine, sine = waves(index, index)
    y_turn = jnp.stack([jnp.stack([cosine, -sine]), jnp.stack([sine, cosine])])
    in_y = jnp.einsum("dcky,cxkz->dxyz", y_turn, volume, precision=HIGH)
    z_turn = jnp.stack([cosine, -sine])
    scores = jnp.einsum("dxyz,dzt->xyt", in_y, z_turn, precision=HIGH)
    summed = scores.reshape(1, slab, GRID * GRID)
    return lax.psum_scatter(summed, "chan", scatter_dimension=2, tiled=True)


def solution(mesh):
    in_specs = (
        P(("grp", "rec")),
        P(),
        P(None, "grp"),
        P("grp"),
        P(None, "chan"),
        P("rec", "chan", None, None, "fft"),
    )
    out_specs = P(("grp", "rec"), "fft", "chan")
    return jax.shard_map(body, mesh=mesh, in_specs=in_specs, out_specs=out_specs, check_vma=False)
```

time: 229 us -> 113 us (0.49); the launches traced: 226 us -> 113 us
  waiting for transfers between devices: 110 us -> 38.4 us
  local copies, waits for them, and re-layouts: 32.9 us -> 11.5 us
  starting transfers between devices: 16.1 us -> 5.79 us
  blocking collectives: 9.15 us -> 4.58 us
  other arithmetic: 12 us -> 8.17 us
    ppermute x2 -> x3, waiting for transfers between devices: 96.9 us -> 25.5 us  [from_behind(): return lax.ppermute(value, axis, pairs)]
    ppermute x2 -> x3, starting transfers between devices: 16.1 us -> 5.72 us  [from_behind(): return lax.ppermute(value, axis, pairs)]
    unnamed x8 -> x14, local copies, waits for them, and re-layouts: 11.9 us -> 3.03 us
    another operation x4 -> x0, local copies, waits for them, and re-layouts: 8.21 us -> none  [the longest x3 7.4 us: body(): jnp.stack([real_y, imaginary_y], axis=2)]
    all_to_all x4 -> x2, local copies, waits for them, and re-layouts: 7.26 us -> 1.42 us  [body(): lax.all_to_all(turned, 'fft', split_axis=2, concat_axis=3, tiled=True)]
    all_to_all x2 -> x1, blocking collectives: 9.15 us -> 4.58 us  [body(): lax.all_to_all(turned, 'fft', split_axis=2, concat_axis=3, tiled=True)]
    all_to_all x1 -> x0, other arithmetic: 4.03 us -> none  [body(): lax.all_to_all(halves, 'fft', split_axis=4, concat_axis=3, tiled=True)]
    dot_general x23 -> x15, matrix products: 31.7 us -> 30.5 us  [the longest x1 6.94 us: ligand_spectrum(): y_im = jnp.dot(y_hat, y_sin, precision=HIGH)]
  transfers between devices with their start and end apart: 3 -> 5, of which waited for: 3 -> 3; matrix products, arithmetic and copies ran while one was open for 0% -> 30% of each run, Pallas kernels for 0% -> 0%
where the time goes in v1:
time: 113 us
  waiting for transfers between devices  38.4 us (34%)
  matrix products  30.5 us (27%)
  between operations  13.8 us (12%)
  local copies, waits for them, and re-layouts  11.5 us (10%)
  other arithmetic  8.17 us (7%)
  starting transfers between devices  5.79 us (5%)
  blocking collectives  4.58 us (4%)
    ppermute x3, waiting for transfers between devices, from_behind(): return lax.ppermute(value, axis, pairs)  25.5 us
    reduce_scatter x1, waiting for transfers between devices, body(): return lax.psum_scatter(summed, 'chan', scatter_dimension=2, tiled=True)  12.9 us
    dot_general x1, matrix products, ligand_spectrum(): y_im = jnp.dot(y_hat, y_sin, precision=HIGH)  6.94 us
    ppermute x3, starting transfers between devices, from_behind(): return lax.ppermute(value, axis, pairs)  5.72 us
    add x1, other arithmetic, ligand_spectrum(): 0.5 * GRID  5.65 us
    all_to_all x1, blocking collectives, body(): lax.all_to_all(turned, 'fft', split_axis=2, concat_axis=3, tiled=True)  4.58 us
    dot_general x1, matrix products, ligand_spectrum(): z_im = jnp.dot(hats[2], z_sin, precision=HIGH)  3.51 us
    dot_general x1, matrix products, ligand_spectrum(): z_re = jnp.dot(hats[2], z_cos, precision=HIGH)  3.48 us
  transfers between devices with their start and end apart: 5, of which 3 were waited for; matrix products, arithmetic and copies ran while one was open for 30% of the time, Pallas kernels for 0%

profile of v1, /device:TPU:0, one launch (start us, length us, event | category | flops | bytes accessed | tf_op | source)
XLA Modules:
  0.0 112.8 jit_solution(874629847484957911)
XLA Ops:
  6.5 0.0 copy-start
  6.5 0.0 reduce-scatter.2.cloned.1.call-start
  6.5 4.0 %collective-permute-start = (s32[1]{0:T(128)}, s32[1]{0:T(128)}, u32[]{:S(2)}, u32[]{:S(2)}) collective-permute-start(s32[1]{0:T(128)} %param.7), channel_id=1, source_target_pairs={{0,8},{4,12},{8,0},{12,4},{1,9},{5,13},{9,1},{13,5},{2,10},{6,14},... | collective-permute-start | bytes 20 | tf_op jit(solution)/shard_map/ppermute | solution.py:17
  10.6 1.1 slice.117
  11.7 0.1 collective-permute-start.1
  11.8 0.1 fusion.90
  11.9 0.1 fusion.93
  12.1 0.1 fusion.84
  12.2 0.1 fusion.95
  12.4 0.7 reshape.229
  13.1 0.7 convert_multiply_fusion
  13.8 0.0 copy-done
  13.8 1.0 fusion.39
  14.8 0.0 collective-permute-done
  14.8 0.8 convolution_bitcast_fusion
  15.6 0.7 fusion.144
  16.3 5.6 %add_add_fusion = (f32[1,512]{1,0:T(1,128)S(1)}, f32[1,512]{1,0:T(1,128)S(1)}, f32[1,512]{1,0:T(1,128)S(1)}) fusion(f32[]{:T(128)} %bitcast.16, f32[]{:T(128)} %bitcast.15, f32[]{:T(128)} %bitcast.14, f32[3,512]{1,0:T(4,128)S(1)} %convert_multiply_fusion, f32[]{:T(128)} %bitcast.6, f32[]{:T(128)} %bitcast.5, f32[]{:T(128)} %bitcast.4, f32[]{:T(128)} %bitcast.10, ...), kind=kLoop, calls=%fused_computation.134 | loop fusion | flops 9216 | bytes 12324 | tf_op jit(solution)/shard_map/add | solution.py:58
  21.9 3.5 %fusion.19 = f32[512,2048]{1,0:T(8,128)S(1)} fusion(s32[2048]{0:T(1024)S(1)} %fusion.86, f32[512]{0:T(512)S(1)} %bitcast.84), kind=kOutput, calls=%fused_computation.33 | convolution fusion | flops 404619264 | bytes 4204544 | tf_op jit(solution)/shard_map/dot_general | solution.py:74
  25.4 3.5 %fusion.23 = f32[512,2048]{1,0:T(8,128)S(1)} fusion(s32[2048]{0:T(1024)S(1)} %fusion.86, f32[512]{0:T(512)S(1)} %bitcast.85), kind=kOutput, calls=%fused_computation.37 | convolution fusion | flops 404619264 | bytes 4204544 | tf_op jit(solution)/shard_map/dot_general | solution.py:73
  28.9 0.4 fusion.38
  29.4 3.5 %fusion.27 = f32[512,2048]{1,0:T(8,128)S(1)} fusion(s32[2048]{0:T(1024)S(1)} %fusion.98, f32[512]{0:T(512)S(1)} %bitcast.88, f32[512]{0:T(512)S(1)} %bitcast.86), kind=kOutput, calls=%fused_computation.41 | convolution fusion | flops 404652032 | bytes 4206592 | tf_op jit(solution)/shard_map/dot_general | solution.py:71
  33.1 0.0 copy-start.3
  33.1 6.9 %multiply_subtract_fusion = (f32[512,2048]{1,0:T(8,128)}, f32[512,2048]{1,0:T(8,128)}) fusion(f32[512,2048]{1,0:T(8,128)S(1)} %fusion.19, f32[512,2048]{1,0:T(8,128)S(1)} %fusion.27, f32[512,2048]{1,0:T(8,128)S(1)} %fusion.23, s32[2048]{0:T(1024)S(1)} %fusion.98, f32[512]{0:T(512)S(1)} %bitcast.89, f32[512]{0:T(512)S(1)} %bitcast.87), kind=kOutput, calls=%fused_computation.1 | convolution fusion | flops 410943488 | bytes 20983808 | tf_op jit(solution)/shard_map/dot_general | solution.py:72
  40.0 0.0 collective-permute-done.1
  40.0 0.0 copy-done.3
  40.0 0.1 broadcast_select_fusion
  40.1 0.2 slice.119
  40.3 0.2 slice.121
  40.5 1.3 %reverse.4 = f32[2,32,2048]{2,1,0:T(8,128)S(1)} reverse(f32[2,32,2048]{2,1,0:T(8,128)S(1)} %bitcast.83), dimensions={1,2} | reverse | bytes 1048576
  41.8 0.2 slice.145
  42.0 1.3 %reverse.5 = f32[2,32,2048]{2,1,0:T(8,128)S(1)} reverse(f32[2,32,2048]{2,1,0:T(8,128)S(1)} %bitcast.82), dimensions={1,2} | reverse | bytes 1048576
  43.3 0.2 slice.146
  43.5 0.1 slice.103
  43.6 0.1 slice.107
  43.7 0.0 copy-done.4
  43.7 0.4 fusion.18
  44.0 0.0 copy-start.2
  44.1 0.1 slice_add_fusion
  44.2 0.4 copy.11
  44.6 1.6 %collective-permute-start.2 = (f32[2,33,2048]{2,0,1:T(2,128)S(1)}, f32[2,33,2048]{2,0,1:T(2,128)S(1)}, u32[]{:S(2)}, u32[]{:S(2)}) collective-permute-start(f32[2,33,2048]{2,0,1:T(2,128)S(1)} %copy.11), channel_id=1, source_target_pairs={{0,4},{4,8},{8,12},{12,0},{1,5},{5,9},{9,13},{13,1},{2,6},{6,10},{... | collective-permute-start | bytes 1622024 | tf_op jit(solution)/shard_map/ppermute | solution.py:17
  46.2 0.0 copy-done.1
  46.2 1.5 %fusion.145 = f32[33,2048]{1,0:T(8,128)S(1)} fusion(f32[33,512]{1,0:T(8,128)S(1)} %fusion.38, f32[512,2048]{1,0:T(8,128)S(1)} %copy-done.1), kind=kOutput, calls=%fused_computation.182 | convolution fusion | flops 207618048 | bytes 4532224 | tf_op jit(solution)/shard_map/dot_general | solution.py:79
  47.7 0.0 copy-done.2
  47.7 1.5 %fusion.146 = f32[33,2048]{1,0:T(8,128)S(1)} fusion(f32[33,512]{1,0:T(8,128)S(1)} %fusion.38, f32[512,2048]{1,0:T(8,128)S(1)} %copy-done.2), kind=kOutput, calls=%fused_computation.183 | convolution fusion | flops 207618048 | bytes 4532224 | tf_op jit(solution)/shard_map/dot_general | solution.py:80
  49.3 11.8 %collective-permute-done.2 = f32[2,33,2048]{2,0,1:T(2,128)S(1)} collective-permute-done((f32[2,33,2048]{2,0,1:T(2,128)S(1)}, f32[2,33,2048]{2,0,1:T(2,128)S(1)}, u32[]{:S(2)}, u32[]{:S(2)}) %collective-permute-start.2) | collective-permute-done | bytes 540704 | tf_op jit(solution)/shard_map/ppermute | solution.py:17
  61.1 0.4 copy_add_fusion.1
  61.4 0.4 copy.13
  61.9 0.1 collective-permute-start.3
  61.9 0.4 fusion.37
  62.4 1.5 %convolution_subtract_fusion = f32[33,2048]{1,0:T(8,128)S(1)} fusion(f32[33,2048]{1,0:T(8,128)S(1)} %fusion.145, f32[33,512]{1,0:T(8,128)S(1)} %fusion.37, f32[512,2048]{1,0:T(8,128)S(1)} %copy-done.2), kind=kOutput, calls=%fused_computation.3 | convolution fusion | flops 207685632 | bytes 4802560 | tf_op jit(solution)/shard_map/dot_general | solution.py:79
  63.9 13.7 %collective-permute-done.3 = f32[2,33,2048]{2,0,1:T(2,128)S(1)} collective-permute-done((f32[2,33,2048]{2,0,1:T(2,128)S(1)}, f32[2,33,2048]{2,0,1:T(2,128)S(1)}, u32[]{:S(2)}, u32[]{:S(2)}) %collective-permute-start.3) | collective-permute-done | bytes 540704 | tf_op jit(solution)/shard_map/ppermute | solution.py:17
  77.6 0.3 copy_add_fusion
  77.9 1.6 %multiply_subtract_fusion.1 = (f32[33,2048]{1,0:T(8,128)S(1)}, f32[33,2048]{1,0:T(8,128)S(1)}) fusion(f32[33,2048]{1,0:T(8,128)S(1)} %convolution_subtract_fusion, f32[2,33,2048]{2,1,0:T(8,128)S(1)} %copy_add_fusion, f32[33,2048]{1,0:T(8,128)S(1)} %fusion.146, f32[33,512]{1,0:T(8,128)S(1)} %fusion.37, f32[512,2048]{1,0:T(8,128)S(1)} %copy-done.1), kind=kOutput, calls=%fused_computation.50 | convolution fusion | flops 208091136 | bytes 5883904 | tf_op jit(solution)/shard_map/dot_general | solution.py:80
  79.5 0.6 fusion.7
  80.1 0.8 copy.15
  80.9 4.6 %all_to_all.15 = f32[1,2,64,2048]{3,1,0,2:T(2,128)S(1)} all-to-all(f32[1,2,64,2048]{3,1,0,2:T(2,128)S(1)} %copy.15), channel_id=1, replica_groups=mesh['grp'=2,'rec'=4,'chan'=2,'fft'=2] {'fft'}, dimensions={2} | all-to-all | bytes 2097152 | tf_op jit(solution)/shard_map/all_to_all | solution.py:111
  85.5 0.6 copy.16
  86.1 0.8 copy.17
  86.9 1.2 %reshape.232 = f32[2,32,64,64]{3,2,1,0:T(8,128)S(1)} reshape(f32[1,2,32,2,2048]{4,3,2,1,0:T(2,128)S(1)} %copy.17) | data formatting | bytes 2097152 | tf_op jit(solution)/shard_map/reshape | solution.py:112
  88.1 1.9 %fusion.2 = f32[32,64,2,64,1]{3,1,4,2,0:T(8,128)S(1)} fusion(f32[1,2,64,64]{3,2,1,0:T(8,128)S(1)} %get-tuple-element.10, f32[1,2,64,64]{3,2,1,0:T(8,128)S(1)} %get-tuple-element.9, f32[2,32,64,64]{3,2,1,0:T(8,128)S(1)} %reshape.232), kind=kOutput, calls=%fused_computation.6 | convolution fusion | flops 201342976 | bytes 2162688 | tf_op jit(solution)/shard_map/dcky,cxkz->dxyz/dot_general | solution.py:115
  90.0 1.8 %fusion.4 = f32[32,64,64]{2,1,0:T(8,128)S(1)} fusion(f32[32,64,2,64,1]{3,1,4,2,0:T(8,128)S(1)} %fusion.2, f32[1,64,64]{2,1,0:T(8,128)S(1)} %fusion.95, f32[1,64,64]{2,1,0:T(8,128)S(1)} %get-tuple-element.26), kind=kOutput, calls=%fused_computation.8 | convolution fusion | flops 100671488 | bytes 1605632 | tf_op jit(solution)/shard_map/dxyz,dzt->xyt/dot_general | solution.py:117
  91.8 1.2 %reshape.233 = f32[1,32,4096]{2,1,0:T(8,128)} reshape(f32[32,64,64]{2,1,0:T(8,128)S(1)} %fusion.4) | data formatting | bytes 1048576 | tf_op jit(solution)/shard_map/reshape | solution.py:118
  93.0 0.0 reduce-scatter.2.cloned.1.call-update
  93.0 12.9 %reduce-scatter.2.cloned.1.call-done = f32[1,32,2048]{2,1,0:T(8,128)} async-done(((f32[1,32,4096]{2,1,0:T(8,128)}), f32[1,32,2048]{2,1,0:T(8,128)}) %reduce-scatter.2.cloned.1.call-update) | async-done | bytes 262160 | tf_op jit(solution)/shard_map/reduce_scatter | solution.py:119
  (9 shorter events, 0.1 us)
Async XLA Ops:
  6.5 7.2 %copy-start = (f32[18,1]{0,1:T(1,128)S(1)}, f32[18,1]{0,1:T(1,128)}, u32[]{:S(2)}) copy-start(f32[18,1]{0,1:T(1,128)} %param.11) | copy-start | bytes 220
  6.5 99.4 %reduce-scatter.2.cloned.1.call-start = ((), (), s32[]{:S(2)}) async-start(), calls=%async_computation.2 | async-start | bytes 786432 | tf_op jit(solution)/shard_map/reduce_scatter | solution.py:119
  6.5 8.3 %collective-permute-start = (s32[1]{0:T(128)}, s32[1]{0:T(128)}, u32[]{:S(2)}, u32[]{:S(2)}) collective-permute-start(s32[1]{0:T(128)} %param.7), channel_id=1, source_target_pairs={{0,8},{4,12},{8,0},{12,4},{1,9},{5,13},{9,1},{13,5},{2,10},{6,14},... | collective-permute-start | bytes 20 | tf_op jit(solution)/shard_map/ppermute | solution.py:17
  11.7 28.4 %collective-permute-start.1 = (f32[2,32,2048]{2,1,0:T(8,128)S(1)}, f32[2,32,2048]{2,1,0:T(8,128)S(1)}, u32[]{:S(2)}, u32[]{:S(2)}) collective-permute-start(f32[2,32,2048]{2,1,0:T(8,128)S(1)} %slice.117), channel_id=1, source_target_pairs={{0,1},{1,0},{2,3},{3,2},{4,5},{5,4},{6,7},{7,6},{8,9},{9,8},{10,11... | collective-permute-start | bytes 1572872 | tf_op jit(solution)/shard_map/ppermute | solution.py:33
  33.1 7.0 %copy-start.3 = (f32[1,1,2,64,2048]{4,3,2,1,0:T(8,128)S(1)}, f32[1,1,2,64,2048]{4,3,2,1,0:T(8,128)}, u32[]{:S(2)}) copy-start(f32[1,1,2,64,2048]{4,3,2,1,0:T(8,128)} %param.12) | copy-start | bytes 3145732
  40.0 3.7 %copy-start.4 = (f32[2]{0:T(128)S(1)}, f32[2]{0:T(128)}, u32[]{:S(2)}) copy-start(f32[2]{0:T(128)} %constant.95.clone) | copy-start | bytes 28
  43.7 2.5 %copy-start.1 = (f32[512,2048]{1,0:T(8,128)S(1)}, f32[512,2048]{1,0:T(8,128)}, u32[]{:S(2)}) copy-start(f32[512,2048]{1,0:T(8,128)} %get-tuple-element.5) | copy-start | bytes 12582916
  44.0 3.7 %copy-start.2 = (f32[512,2048]{1,0:T(8,128)S(1)}, f32[512,2048]{1,0:T(8,128)}, u32[]{:S(2)}) copy-start(f32[512,2048]{1,0:T(8,128)} %get-tuple-element.6) | copy-start | bytes 12582916
  44.6 16.5 %collective-permute-start.2 = (f32[2,33,2048]{2,0,1:T(2,128)S(1)}, f32[2,33,2048]{2,0,1:T(2,128)S(1)}, u32[]{:S(2)}, u32[]{:S(2)}) collective-permute-start(f32[2,33,2048]{2,0,1:T(2,128)S(1)} %copy.11), channel_id=1, source_target_pairs={{0,4},{4,8},{8,12},{12,0},{1,5},{5,9},{9,13},{13,1},{2,6},{6,10},{... | collective-permute-start | bytes 1622024 | tf_op jit(solution)/shard_map/ppermute | solution.py:17
  61.9 15.7 %collective-permute-start.3 = (f32[2,33,2048]{2,0,1:T(2,128)S(1)}, f32[2,33,2048]{2,0,1:T(2,128)S(1)}, u32[]{:S(2)}, u32[]{:S(2)}) collective-permute-start(f32[2,33,2048]{2,0,1:T(2,128)S(1)} %copy.13), channel_id=1, source_target_pairs={{0,4},{4,8},{8,12},{12,0},{1,5},{5,9},{9,13},{13,1},{2,6},{6,10},{... | collective-permute-start | bytes 1622024 | tf_op jit(solution)/shard_map/ppermute | solution.py:17
Sparse Core Ops, SparseCore 0:
  93.1 12.7 reduce-scatter.1

commit v2 on v1

--- a/solution.py
+++ b/solution.py
@@ -86,11 +86,12 @@
     slab = GRID // lax.axis_size("fft")
     record = from_behind(record_ids, "rec", 2)
     folded = fold(receptor_spectra[0, 0], width)
+    folded, record, coords, types, weights = lax.optimization_barrier(
+        (folded, record, ligand_coords, atom_types, channel_weights)
+    )
     pair = folded + from_behind(folded, "rec", 1)
     window = folded + from_behind(pair, "rec", 1)
-    lig_re, lig_im = ligand_spectrum(
-        record, rotations, ligand_coords, atom_types, channel_weights, width
-    )
+    lig_re, lig_im = ligand_spectrum(record, rotations, coords, types, weights, width)
     product_re = lig_re * window[0] - lig_im * window[1]
     product_im = lig_re * window[1] + lig_im * window[0]
     index = jnp.arange(GRID, dtype=jnp.int32)
@@ -111,12 +112,22 @@
     halves = lax.all_to_all(turned, "fft", split_axis=2, concat_axis=3, tiled=True)
     volume = halves.reshape(2, slab, GRID, GRID)
     cosine, sine = waves(index, index)
-    y_turn = jnp.stack([jnp.stack([cosine, -sine]), jnp.stack([sine, cosine])])
-    in_y = jnp.einsum("dcky,cxkz->dxyz", y_turn, volume, precision=HIGH)
     z_turn = jnp.stack([cosine, -sine])
-    scores = jnp.einsum("dxyz,dzt->xyt", in_y, z_turn, precision=HIGH)
-    summed = scores.reshape(1, slab, GRID * GRID)
-    return lax.psum_scatter(summed, "chan", scatter_dimension=2, tiled=True)
+
+    def scores(places):
+        y_cos, y_sin = waves(index, places)
+        y_turn = jnp.stack([jnp.stack([y_cos, -y_sin]), jnp.stack([y_sin, y_cos])])
+        in_y = jnp.einsum("dcky,cxkz->dxyz", y_turn, volume, precision=HIGH)
+        part = jnp.einsum("dxyz,dzt->xyt", in_y, z_turn, precision=HIGH)
+        return part.reshape(1, slab, places.shape[0] * GRID)
+
+    count = lax.axis_size("chan")
+    if count != 2:
+        return lax.psum_scatter(scores(index), "chan", scatter_dimension=2, tiled=True)
+    near = lax.axis_index("chan") * HALF + jnp.arange(HALF, dtype=jnp.int32)
+    far = (near + HALF) % GRID
+    arrived = from_behind(scores(far), "chan", 1)
+    return scores(near) + arrived
 
 
 def solution(mesh):

time: 113 us -> 81.2 us (0.72)
  waiting for transfers between devices: 38.4 us -> 21.9 us
  between operations: 13.8 us -> 0.31 us
  matrix products: 30.5 us -> 26.1 us
  starting transfers between devices: 5.79 us -> 7.82 us
  other arithmetic: 8.17 us -> 9.42 us
    reduce_scatter x1 -> x0, waiting for transfers between devices: 12.9 us -> none  [body(): return lax.psum_scatter(summed, 'chan', scatter_dimension=2, tiled=True)]
    ppermute x3 -> x4, waiting for transfers between devices: 25.5 us -> 21.9 us  [from_behind(): return lax.ppermute(value, axis, pairs)]
    dot_general x1, matrix products: 6.94 us -> 4.42 us  [ligand_spectrum(): y_im = jnp.dot(y_hat, y_sin, precision=HIGH)]
    ppermute x3 -> x4, starting transfers between devices: 5.72 us -> 7.31 us  [from_behind(): return lax.ppermute(value, axis, pairs)]
    dot_general x2 -> x4, matrix products: 3.68 us -> 2.57 us  [the longest x2 1.38 us: scores(): in_y = jnp.einsum('dcky,cxkz->dxyz', y_turn, volume, precision=HIGH)]
  transfers between devices with their start and end apart: 5 -> 5, of which waited for: 3 -> 3; matrix products, arithmetic and copies ran while one was open for 30% -> 26% of each run, Pallas kernels for 0% -> 0%
where the time goes in v2:
time: 81.2 us; the launch traced here: 80.9 us
  matrix products  26.1 us (32%)
  waiting for transfers between devices  21.9 us (27%)
  local copies, waits for them, and re-layouts  10.7 us (13%)
  other arithmetic  9.42 us (12%)
  starting transfers between devices  7.82 us (10%)
  blocking collectives  4.58 us (6%)
    ppermute x4, waiting for transfers between devices, from_behind(): return lax.ppermute(value, axis, pairs)  21.9 us
    ppermute x4, starting transfers between devices, from_behind(): return lax.ppermute(value, axis, pairs)  7.31 us
    add x1, other arithmetic, ligand_spectrum(): 0.5 * GRID  5.65 us
    all_to_all x1, blocking collectives, body(): lax.all_to_all(turned, 'fft', split_axis=2, concat_axis=3, tiled=True)  4.58 us
    dot_general x1, matrix products, ligand_spectrum(): y_im = jnp.dot(y_hat, y_sin, precision=HIGH)  4.42 us
    dot_general x1, matrix products, ligand_spectrum(): z_im = jnp.dot(hats[2], z_sin, precision=HIGH)  3.51 us
    dot_general x1, matrix products, ligand_spectrum(): y_re = jnp.dot(y_hat, y_cos, precision=HIGH)  3.49 us
    dot_general x1, matrix products, ligand_spectrum(): z_re = jnp.dot(hats[2], z_cos, precision=HIGH)  3.48 us
  transfers between devices with their start and end apart: 5, of which 3 were waited for; matrix products, arithmetic and copies ran while one was open for 26% of the time, Pallas kernels for 0%

profile of v2, /device:TPU:0, one launch (start us, length us, event | category | flops | bytes accessed | tf_op | source)
XLA Modules:
  0.0 80.9 jit_solution(1526344427914244700)
XLA Ops:
  0.0 1.1 %slice.114 = f32[2,32,2048]{2,1,0:T(8,128)S(1)} slice(f32[2,64,2048]{2,1,0:T(8,128)} %bitcast.98), slice={[0:2], [32:64], [0:2048]} | slice | bytes 1048576 | tf_op jit(solution)/shard_map/slice | solution.py:32
  1.1 0.5 collective-permute-start
  1.6 3.7 %collective-permute-start.1 = (s32[1]{0:T(128)}, s32[1]{0:T(128)}, u32[]{:S(2)}, u32[]{:S(2)}) collective-permute-start(s32[1]{0:T(128)} %param.7), channel_id=1, source_target_pairs={{0,8},{4,12},{8,0},{12,4},{1,9},{5,13},{9,1},{13,5},{2,10},{6,14},... | collective-permute-start | bytes 20 | tf_op jit(solution)/shard_map/ppermute | solution.py:17
  5.3 0.1 fusion.98
  5.4 0.1 fusion.101
  5.6 0.1 sine_negate_fusion
  5.7 0.7 reshape.495
  6.5 0.2 fusion.116
  6.6 0.0 copy-start.3
  6.7 0.2 fusion.115
  6.8 0.0 collective-permute-done
  6.8 1.1 %broadcast_select_fusion = f32[2,32,2048]{2,1,0:T(8,128)S(1)} fusion(f32[2,32,2048]{2,1,0:T(8,128)S(1)} %collective-permute-done, pred[2048]{0:T(1024)(128)(4,1)S(1)} %iota_compare_fusion.2, f32[2,64,2048]{2,1,0:T(8,128)} %bitcast.99), kind=kLoop, calls=%fused_computation.60 | loop fusion | flops 131072 | bytes 1574912 | tf_op jit(solution)/shard_map/jit(_where)/select_n | solution.py:34
  8.0 0.0 copy-start.1
  8.0 0.2 slice.116
  8.2 0.2 slice.118
  8.4 1.3 %reverse.4 = f32[2,32,2048]{2,1,0:T(8,128)S(1)} reverse(f32[2,32,2048]{2,1,0:T(8,128)S(1)} %bitcast.102), dimensions={1,2} | reverse | bytes 1048576
  9.7 0.2 slice.145
  9.9 1.3 %reverse.5 = f32[2,32,2048]{2,1,0:T(8,128)S(1)} reverse(f32[2,32,2048]{2,1,0:T(8,128)S(1)} %bitcast.101), dimensions={1,2} | reverse | bytes 1048576
  11.2 0.2 slice.146
  11.4 0.1 slice.91
  11.5 0.1 slice.95
  11.6 0.4 fusion.21
  12.0 0.0 copy-done.1
  12.0 0.1 slice_add_fusion
  12.1 0.0 collective-permute-done.1
  12.1 0.7 convolution_bitcast_fusion.2
  12.7 0.7 fusion.164
  13.5 0.0 copy-done.2
  13.5 5.6 %add_add_fusion = (f32[1,512]{1,0:T(1,128)S(1)}, f32[1,512]{1,0:T(1,128)S(1)}, f32[1,512]{1,0:T(1,128)S(1)}) fusion(f32[]{:T(128)} %bitcast.17, f32[]{:T(128)} %bitcast.16, f32[]{:T(128)} %bitcast.15, f32[3,512]{1,0:T(4,128)S(1)} %convert_multiply_fusion, f32[]{:T(128)} %bitcast.7, f32[]{:T(128)} %bitcast.6, f32[]{:T(128)} %bitcast.5, f32[]{:T(128)} %bitcast.11, ...), kind=kLoop, calls=%fused_computation.165 | loop fusion | flops 9216 | bytes 12324 | tf_op jit(solution)/shard_map/add | solution.py:58
  19.1 0.0 copy-start.4
  19.1 3.5 %fusion.22 = f32[512,2048]{1,0:T(8,128)S(1)} fusion(s32[2048]{0:T(1024)S(1)} %add_select_fusion.7, f32[512]{0:T(512)S(1)} %bitcast.103), kind=kOutput, calls=%fused_computation.36 | convolution fusion | flops 404619264 | bytes 4204544 | tf_op jit(solution)/shard_map/dot_general | solution.py:74
  22.7 3.5 %fusion.26 = f32[512,2048]{1,0:T(8,128)S(1)} fusion(s32[2048]{0:T(1024)S(1)} %add_select_fusion.7, f32[512]{0:T(512)S(1)} %bitcast.104), kind=kOutput, calls=%fused_computation.40 | convolution fusion | flops 404619264 | bytes 4204544 | tf_op jit(solution)/shard_map/dot_general | solution.py:73
  26.1 0.4 fusion.41
  26.6 0.4 copy.11
  27.0 1.8 %collective-permute-start.2 = (f32[2,33,2048]{2,0,1:T(2,128)S(1)}, f32[2,33,2048]{2,0,1:T(2,128)S(1)}, u32[]{:S(2)}, u32[]{:S(2)}) collective-permute-start(f32[2,33,2048]{2,0,1:T(2,128)S(1)} %copy.11), channel_id=1, source_target_pairs={{0,4},{4,8},{8,12},{12,0},{1,5},{5,9},{9,13},{13,1},{2,6},{6,10},{... | collective-permute-start | bytes 1622024 | tf_op jit(solution)/shard_map/ppermute | solution.py:17
  28.8 0.3 fusion.42
  29.1 3.5 %fusion.30 = f32[512,2048]{1,0:T(8,128)S(1)} fusion(s32[2048]{0:T(1024)S(1)} %fusion.106, f32[512]{0:T(512)S(1)} %bitcast.107, f32[512]{0:T(512)S(1)} %bitcast.105), kind=kOutput, calls=%fused_computation.44 | convolution fusion | flops 404652032 | bytes 4206592 | tf_op jit(solution)/shard_map/dot_general | solution.py:71
  32.7 4.4 %multiply_subtract_fusion = (f32[512,2048]{1,0:T(8,128)S(1)}, f32[512,2048]{1,0:T(8,128)S(1)}) fusion(f32[512,2048]{1,0:T(8,128)S(1)} %fusion.22, f32[512,2048]{1,0:T(8,128)S(1)} %fusion.30, f32[512,2048]{1,0:T(8,128)S(1)} %fusion.26, s32[2048]{0:T(1024)S(1)} %fusion.106, f32[512]{0:T(512)S(1)} %bitcast.108, f32[512]{0:T(512)S(1)} %bitcast.106), kind=kOutput, calls=%fused_computation.1 | convolution fusion | flops 410943488 | bytes 20983808 | tf_op jit(solution)/shard_map/dot_general | solution.py:72
  37.1 1.5 %fusion.166 = f32[33,2048]{1,0:T(8,128)S(1)} fusion(f32[33,512]{1,0:T(8,128)S(1)} %fusion.41, f32[512,2048]{1,0:T(8,128)S(1)} %get-tuple-element.16), kind=kOutput, calls=%fused_computation.219 | convolution fusion | flops 207618048 | bytes 4532224 | tf_op jit(solution)/shard_map/dot_general | solution.py:80
  38.6 1.5 %fusion.165 = f32[33,2048]{1,0:T(8,128)S(1)} fusion(f32[33,512]{1,0:T(8,128)S(1)} %fusion.41, f32[512,2048]{1,0:T(8,128)S(1)} %get-tuple-element.15), kind=kOutput, calls=%fused_computation.218 | convolution fusion | flops 207618048 | bytes 4532224 | tf_op jit(solution)/shard_map/dot_general | solution.py:79
  40.1 3.3 %collective-permute-done.2 = f32[2,33,2048]{2,0,1:T(2,128)S(1)} collective-permute-done((f32[2,33,2048]{2,0,1:T(2,128)S(1)}, f32[2,33,2048]{2,0,1:T(2,128)S(1)}, u32[]{:S(2)}, u32[]{:S(2)}) %collective-permute-start.2) | collective-permute-done | bytes 540704 | tf_op jit(solution)/shard_map/ppermute | solution.py:17
  43.4 0.3 copy_add_fusion.1
  43.7 0.4 copy.13
  44.2 0.3 collective-permute-start.3
  44.5 0.4 fusion.40
  44.9 1.5 %convolution_subtract_fusion = f32[33,2048]{1,0:T(8,128)S(1)} fusion(f32[33,2048]{1,0:T(8,128)S(1)} %fusion.165, f32[33,512]{1,0:T(8,128)S(1)} %fusion.40, f32[512,2048]{1,0:T(8,128)S(1)} %get-tuple-element.16), kind=kOutput, calls=%fused_computation.3 | convolution fusion | flops 207685632 | bytes 4802560 | tf_op jit(solution)/shard_map/dot_general | solution.py:79
  46.4 13.3 %collective-permute-done.3 = f32[2,33,2048]{2,0,1:T(2,128)S(1)} collective-permute-done((f32[2,33,2048]{2,0,1:T(2,128)S(1)}, f32[2,33,2048]{2,0,1:T(2,128)S(1)}, u32[]{:S(2)}, u32[]{:S(2)}) %collective-permute-start.3) | collective-permute-done | bytes 540704 | tf_op jit(solution)/shard_map/ppermute | solution.py:17
  59.8 0.3 copy_add_fusion
  60.1 1.6 %multiply_subtract_fusion.1 = (f32[33,2048]{1,0:T(8,128)S(1)}, f32[33,2048]{1,0:T(8,128)S(1)}) fusion(f32[33,2048]{1,0:T(8,128)S(1)} %convolution_subtract_fusion, f32[2,33,2048]{2,1,0:T(8,128)S(1)} %copy_add_fusion, f32[33,2048]{1,0:T(8,128)S(1)} %fusion.166, f32[33,512]{1,0:T(8,128)S(1)} %fusion.40, f32[512,2048]{1,0:T(8,128)S(1)} %get-tuple-element.15), kind=kOutput, calls=%fused_computation.53 | convolution fusion | flops 208091136 | bytes 5883904 | tf_op jit(solution)/shard_map/dot_general | solution.py:80
  61.7 0.6 fusion.10
  62.3 0.8 %copy.15 = f32[1,2,64,2048]{3,1,0,2:T(2,128)S(1)} copy(f32[1,2,64,2048]{3,2,1,0:T(8,128)S(1)} %bitcast.96) | data formatting | bytes 2097152 | tf_op jit(solution)/shard_map/reshape | solution.py:111
  63.1 4.6 %all_to_all.15 = f32[1,2,64,2048]{3,1,0,2:T(2,128)S(1)} all-to-all(f32[1,2,64,2048]{3,1,0,2:T(2,128)S(1)} %copy.15), channel_id=1, replica_groups=mesh['grp'=2,'rec'=4,'chan'=2,'fft'=2] {'fft'}, dimensions={2} | all-to-all | bytes 2097152 | tf_op jit(solution)/shard_map/all_to_all | solution.py:112
  67.7 0.6 copy.16
  68.3 0.8 %copy.17 = f32[1,2,32,2,2048]{4,3,2,1,0:T(2,128)S(1)} copy(f32[1,2,32,2,2048]{4,2,3,1,0:T(8,128)S(1)} %bitcast.97) | data formatting | bytes 2097152 | tf_op jit(solution)/shard_map/all_to_all | solution.py:112
  69.1 1.2 %reshape.498 = f32[2,32,64,64]{3,2,1,0:T(8,128)S(1)} reshape(f32[1,2,32,2,2048]{4,3,2,1,0:T(2,128)S(1)} %copy.17) | data formatting | bytes 2097152 | tf_op jit(solution)/shard_map/reshape | solution.py:113
  70.3 0.7 fusion.7
  71.0 0.6 convolution_bitcast_fusion
  71.6 0.2 reshape.500
  71.8 1.6 %collective-permute-start.4 = (f32[1,32,2048]{2,1,0:T(8,128)S(1)}, f32[1,32,2048]{2,1,0:T(8,128)S(1)}, u32[]{:S(2)}, u32[]{:S(2)}) collective-permute-start(f32[1,32,2048]{2,1,0:T(8,128)S(1)} %reshape.500), channel_id=1, source_target_pairs={{0,2},{2,0},{1,3},{3,1},{4,6},{6,4},{5,7},{7,5},{8,10},{10,8},{9,1... | collective-permute-start | bytes 786440 | tf_op jit(solution)/shard_map/ppermute | solution.py:17
  73.3 0.7 fusion.4
  74.0 0.6 convolution_bitcast_fusion.1
  74.6 0.2 reshape.499
  74.8 5.4 %collective-permute-done.4 = f32[1,32,2048]{2,1,0:T(8,128)S(1)} collective-permute-done((f32[1,32,2048]{2,1,0:T(8,128)S(1)}, f32[1,32,2048]{2,1,0:T(8,128)S(1)}, u32[]{:S(2)}, u32[]{:S(2)}) %collective-permute-start.4) | collective-permute-done | bytes 262176 | tf_op jit(solution)/shard_map/ppermute | solution.py:17
  80.2 0.7 add.286
  (15 shorter events, 0.1 us)
Async XLA Ops:
  0.0 28.8 %copy-start = (f32[18,1]{0,1:T(1,128)S(1)}, f32[18,1]{0,1:T(1,128)}, u32[]{:S(2)}) copy-start(f32[18,1]{0,1:T(1,128)} %param.11) | copy-start | bytes 220
  1.1 5.7 %collective-permute-start = (f32[2,32,2048]{2,1,0:T(8,128)S(1)}, f32[2,32,2048]{2,1,0:T(8,128)S(1)}, u32[]{:S(2)}, u32[]{:S(2)}) collective-permute-start(f32[2,32,2048]{2,1,0:T(8,128)S(1)} %slice.114), channel_id=1, source_target_pairs={{0,1},{1,0},{2,3},{3,2},{4,5},{5,4},{6,7},{7,6},{8,9},{9,8},{10,11... | collective-permute-start | bytes 1572872 | tf_op jit(solution)/shard_map/ppermute | solution.py:33
  1.6 10.4 %collective-permute-start.1 = (s32[1]{0:T(128)}, s32[1]{0:T(128)}, u32[]{:S(2)}, u32[]{:S(2)}) collective-permute-start(s32[1]{0:T(128)} %param.7), channel_id=1, source_target_pairs={{0,8},{4,12},{8,0},{12,4},{1,9},{5,13},{9,1},{13,5},{2,10},{6,14},... | collective-permute-start | bytes 20 | tf_op jit(solution)/shard_map/ppermute | solution.py:17
  6.6 5.0 %copy-start.3 = (f32[2]{0:T(128)S(1)}, f32[2]{0:T(128)}, u32[]{:S(2)}) copy-start(f32[2]{0:T(128)} %constant.120.clone) | copy-start | bytes 28
  8.0 4.0 %copy-start.1 = (f32[1,1,2,64,2048]{4,3,2,1,0:T(8,128)S(1)}, f32[1,1,2,64,2048]{4,3,2,1,0:T(8,128)}, u32[]{:S(2)}) copy-start(f32[1,1,2,64,2048]{4,3,2,1,0:T(8,128)} %param.12) | copy-start | bytes 3145732
  8.4 5.1 %copy-start.2 = (s32[3,512]{1,0:T(4,128)S(1)}, s32[3,512]{1,0:T(4,128)}, u32[]{:S(2)}) copy-start(s32[3,512]{1,0:T(4,128)} %param.9) | copy-start | bytes 18436
  19.1 9.7 %copy-start.4 = (s32[512]{0:T(512)S(1)}, s32[512]{0:T(512)}, u32[]{:S(2)}) copy-start(s32[512]{0:T(512)} %param.10) | copy-start | bytes 6148
  27.0 16.4 %collective-permute-start.2 = (f32[2,33,2048]{2,0,1:T(2,128)S(1)}, f32[2,33,2048]{2,0,1:T(2,128)S(1)}, u32[]{:S(2)}, u32[]{:S(2)}) collective-permute-start(f32[2,33,2048]{2,0,1:T(2,128)S(1)} %copy.11), channel_id=1, source_target_pairs={{0,4},{4,8},{8,12},{12,0},{1,5},{5,9},{9,13},{13,1},{2,6},{6,10},{... | collective-permute-start | bytes 1622024 | tf_op jit(solution)/shard_map/ppermute | solution.py:17
  44.2 15.6 %collective-permute-start.3 = (f32[2,33,2048]{2,0,1:T(2,128)S(1)}, f32[2,33,2048]{2,0,1:T(2,128)S(1)}, u32[]{:S(2)}, u32[]{:S(2)}) collective-permute-start(f32[2,33,2048]{2,0,1:T(2,128)S(1)} %copy.13), channel_id=1, source_target_pairs={{0,4},{4,8},{8,12},{12,0},{1,5},{5,9},{9,13},{13,1},{2,6},{6,10},{... | collective-permute-start | bytes 1622024 | tf_op jit(solution)/shard_map/ppermute | solution.py:17
  71.8 8.4 %collective-permute-start.4 = (f32[1,32,2048]{2,1,0:T(8,128)S(1)}, f32[1,32,2048]{2,1,0:T(8,128)S(1)}, u32[]{:S(2)}, u32[]{:S(2)}) collective-permute-start(f32[1,32,2048]{2,1,0:T(8,128)S(1)} %reshape.500), channel_id=1, source_target_pairs={{0,2},{2,0},{1,3},{3,1},{4,6},{6,4},{5,7},{7,5},{8,10},{10,8},{9,1... | collective-permute-start | bytes 786440 | tf_op jit(solution)/shard_map/ppermute | solution.py:17

commit v3 on v2

v3 whole, which is shorter than its diff:
```python
import math

import functools

import jax
import jax.numpy as jnp
import numpy as np
from jax import lax
from jax.experimental import pallas as pl
from jax.experimental.pallas import tpu as pltpu
from jax.sharding import PartitionSpec as P

GRID = 64
HALF = GRID // 2
HIGHEST = lax.Precision.HIGHEST
HIGH = lax.Precision.HIGH


def from_behind(value, axis, steps):
    count = lax.axis_size(axis)
    pairs = [(source, (source + steps) % count) for source in range(count)]
    return lax.ppermute(value, axis, pairs)


def waves(rows, columns):
    phase = rows[:, None] * columns[None, :] % GRID
    angle = phase.astype(jnp.float32) * (2.0 * math.pi / GRID)
    return jnp.cos(angle), jnp.sin(angle)


def hat_rows(places, cells):
    return jnp.maximum(0.0, 1.0 - jnp.abs(places[:, None] - cells[None, :]))


def fold(receptor, width):
    lane = jnp.arange(width, dtype=jnp.int32)
    upper = receptor[:, HALF:]
    other = lax.ppermute(upper, "fft", [(0, 1), (1, 0)])
    source = jnp.where(lane < GRID, upper, other)
    back = lax.rev(source, (1, 2))
    mirrored = jnp.where(lane % GRID == 0, jnp.roll(back, 1, axis=2), jnp.roll(back, 65, axis=2))
    sign = jnp.array([1.0, -1.0], jnp.float32)[:, None, None]
    inner = mirrored[:, : HALF - 1] * sign
    inner = jnp.pad(inner, ((0, 0), (1, 1), (0, 0)))
    return receptor[:, : HALF + 1] + inner


def host_waves(rows, columns):
    angle = (np.outer(rows, columns) % GRID) * (2.0 * np.pi / GRID)
    return np.cos(angle), np.sin(angle)


def tripled(table):
    table = table.astype(np.float32)
    high = table.astype(jnp.bfloat16)
    low = (table - high.astype(np.float32)).astype(jnp.bfloat16)
    return np.concatenate([high, high, low], axis=0)


ROWS = 72
LANES = 256


def split(value):
    high = value.astype(jnp.bfloat16)
    return high, (value - high.astype(jnp.float32)).astype(jnp.bfloat16)


def dot(left, right):
    return jnp.dot(left, right, preferred_element_type=jnp.float32)


def window_kernel(
    count, g_ref, l_ref, y_ref, z_ref, yt_ref, zt_ref, turn_ref, out_ref,
    own, first, pair, second, win, lig, z_wave, l_high, l_low,
    send1, recv1, send2, recv2, send3, recv3,
):
    grp = lax.axis_index("grp")
    rec = lax.axis_index("rec")
    after = lax.rem(rec + 1, count)
    before = lax.rem(rec + count - 1, count)
    chunks = own.shape[0]
    mine = chunks // 2
    barrier = pltpu.get_barrier_semaphore()
    for target in ({"rec": after}, {"rec": before}, {"grp": 1 - grp}):
        pl.semaphore_signal(
            barrier, inc=1, device_id=target, device_id_type=pl.DeviceIdType.MESH
        )
    for chunk in range(chunks):
        own[chunk] = g_ref[:, chunk * LANES : (chunk + 1) * LANES]
    pl.semaphore_wait(barrier, 3)
    base = grp * mine

    def remote(source, target, send, recv, device):
        return pltpu.make_async_remote_copy(
            src_ref=source, dst_ref=target, send_sem=send, recv_sem=recv,
            device_id=device, device_id_type=pl.DeviceIdType.MESH,
        )

    ones = [
        remote(own.at[base + c], first.at[c], send1.at[c], recv1.at[c], {"rec": after})
        for c in range(mine)
    ]
    twos = [
        remote(pair.at[c], second.at[c], send2.at[c], recv2.at[c], {"rec": after})
        for c in range(mine)
    ]
    threes = [
        remote(win.at[base + c], win.at[base + c], send3.at[c], recv3.at[c], {"grp": 1 - grp})
        for c in range(mine)
    ]
    for copy in ones:
        copy.start()

    z_wave[...] = dot(z_ref[...], zt_ref[...])
    high, low = split(l_ref[...])
    l_high[...] = high
    l_low[...] = low

    def ligand(chunk):
        y_wave = dot(y_ref[...], yt_ref[chunk])
        y_re, y_im = y_wave[:, :LANES], y_wave[:, LANES:]
        z_re, z_im = z_wave[:, :LANES], z_wave[:, LANES:]
        re_high, re_low = split(y_re * z_re - y_im * z_im)
        im_high, im_low = split(y_re * z_im + y_im * z_re)
        v_high = jnp.concatenate([re_high, im_high], axis=0)
        v_low = jnp.concatenate([re_low, im_low], axis=0)
        lig[chunk] = (
            dot(l_high[...], v_high) + dot(l_low[...], v_high) + dot(l_high[...], v_low)
        )

    t_high, t_low = split(turn_ref[...])

    def product(chunk):
        l_re, l_im = lig[chunk, 0:32], lig[chunk, 32:64]
        w_re, w_im = win[chunk, 0:32], win[chunk, 32:64]
        tail_l, tail_w = lig[chunk, 64:72], win[chunk, 64:72]
        a, b = tail_l[0:1], tail_l[1:2]
        c, d = tail_w[0:1], tail_w[1:2]
        row = lax.broadcasted_iota(jnp.int32, (8, LANES), 0)
        tail = jnp.where(row == 0, a * c - b * d, jnp.where(row == 1, a * d + b * c, 0.0))
        whole = jnp.concatenate([l_re * w_re - l_im * w_im, l_re * w_im + l_im * w_re, tail], axis=0)
        p_high, p_low = split(whole)
        lanes = pl.ds(pl.multiple_of(chunk * LANES, LANES), LANES)
        out_ref[:, lanes] = dot(t_high, p_high) + dot(t_low, p_high) + dot(t_high, p_low)

    ligand(0)
    ligand(1)
    ligand(2)
    for c in range(mine):
        ones[c].wait_recv()
        pair[c] = own[base + c] + first[c]
        twos[c].start()
        ligand(3 + c)
    ligand(7)
    for c in range(mine):
        twos[c].wait_recv()
        win[base + c] = own[base + c] + second[c]
        threes[c].start()
        product(base + c)
    for c in range(mine):
        threes[c].wait_recv()
        product((1 - grp) * mine + c)
    for copy in ones + twos + threes:
        copy.wait_send()


def turned_product(folded, left, y_hat, z_hat, width):
    index = np.arange(GRID)
    chunks = width // LANES
    lane = np.arange(width)
    cosine, sine = host_waves(index, lane // GRID)
    y_table = np.stack(
        [
            tripled(
                np.concatenate(
                    [t[:, c * LANES : (c + 1) * LANES] for t in (cosine, sine)], axis=1
                )
            )
            for c in range(chunks)
        ]
    )
    z_table = tripled(np.concatenate(host_waves(index, lane[:LANES] % GRID), axis=1))
    cosine, sine = host_waves(index, np.arange(HALF + 1))
    real = np.concatenate([cosine[:, :HALF], -sine[:, :HALF], cosine[:, HALF:], -sine[:, HALF:]], 1)
    imag = np.concatenate([sine[:, :HALF], cosine[:, :HALF], sine[:, HALF:], cosine[:, HALF:]], 1)
    turn = np.concatenate([real, imag], axis=0) / float(GRID**3)
    turn = np.pad(turn, ((0, 0), (0, ROWS - turn.shape[1]))).astype(np.float32)

    def columns(value):
        high = lax.reduce_precision(value, 8, 7)
        return jnp.concatenate([high, value - high, high], axis=1).astype(jnp.bfloat16)

    atoms = y_hat.shape[0]
    piece = (ROWS, LANES)
    half = chunks // 2
    return pl.pallas_call(
        functools.partial(window_kernel, lax.axis_size("rec")),
        out_shape=jax.ShapeDtypeStruct((2 * GRID, width), jnp.float32),
        in_specs=[pl.BlockSpec(memory_space=pltpu.VMEM)] * 7,
        out_specs=pl.BlockSpec(memory_space=pltpu.VMEM),
        scratch_shapes=[
            pltpu.VMEM((chunks,) + piece, jnp.float32),
            pltpu.VMEM((half,) + piece, jnp.float32),
            pltpu.VMEM((half,) + piece, jnp.float32),
            pltpu.VMEM((half,) + piece, jnp.float32),
            pltpu.VMEM((chunks,) + piece, jnp.float32),
            pltpu.VMEM((chunks,) + piece, jnp.float32),
            pltpu.VMEM((atoms, 2 * LANES), jnp.float32),
            pltpu.VMEM((ROWS, 2 * atoms), jnp.bfloat16),
            pltpu.VMEM((ROWS, 2 * atoms), jnp.bfloat16),
        ]
        + [pltpu.SemaphoreType.DMA((half,))] * 6,
        compiler_params=pltpu.CompilerParams(
            collective_id=0, has_side_effects=True, vmem_limit_bytes=40 * 1024 * 1024
        ),
    )(
        folded, left, columns(y_hat), columns(z_hat),
        jnp.asarray(y_table), jnp.asarray(z_table), jnp.asarray(turn),
    )


def hats_of(record, rotations, ligand_coords, atom_types, channel_weights):
    table_rows = rotations.shape[0]
    picks = (record[:, None] == jnp.arange(table_rows, dtype=jnp.int32)[None, :]).astype(
        jnp.float32
    )
    matrix = jnp.dot(picks, rotations.reshape(table_rows, 9), precision=HIGHEST)[0]
    kinds = channel_weights.shape[0]
    type_hot = (atom_types[:, None] == jnp.arange(kinds, dtype=jnp.int32)[None, :]).astype(
        jnp.float32
    )
    weights = jnp.dot(type_hot, channel_weights, precision=HIGHEST)
    coords = ligand_coords.astype(jnp.float32) * (1.0 / 256.0)
    places = [
        0.5 * GRID
        + (
            matrix[3 * row] * coords[0]
            + matrix[3 * row + 1] * coords[1]
            + matrix[3 * row + 2] * coords[2]
        )
        for row in range(3)
    ]
    cells = jnp.arange(GRID, dtype=jnp.float32)
    odd = (jnp.arange(GRID, dtype=jnp.int32) * lax.axis_index("fft")) % 2
    y_hat = hat_rows(places[1], cells) * weights * (1.0 - 2.0 * odd.astype(jnp.float32))
    z_hat = hat_rows(places[2], cells)
    cosine, sine = host_waves(np.arange(HALF + 1), np.arange(GRID))
    none = np.zeros((6, GRID))
    meet_re = np.concatenate([cosine[:HALF], sine[:HALF], cosine[HALF:], sine[HALF:], none], 0)
    meet_im = np.concatenate([-sine[:HALF], cosine[:HALF], -sine[HALF:], cosine[HALF:], none], 0)
    table = jnp.asarray(np.stack([meet_re, meet_im], axis=1).reshape(2 * ROWS, GRID), jnp.float32)
    x_hat = jnp.maximum(0.0, 1.0 - jnp.abs(places[0][None, :] - cells[:, None]))
    left = jnp.dot(table, x_hat, precision=HIGHEST).reshape(ROWS, 2 * x_hat.shape[1])
    return left, y_hat, z_hat


def body(record_ids, rotations, ligand_coords, atom_types, channel_weights, receptor_spectra):
    width = receptor_spectra.shape[-1]
    slab = GRID // lax.axis_size("fft")
    record = from_behind(record_ids, "rec", 2)
    folded = fold(receptor_spectra[0, 0], width)
    folded = jnp.concatenate(
        [
            folded[:, :HALF].reshape(GRID, width),
            folded[:, HALF],
            jnp.zeros((ROWS - GRID - 2, width), jnp.float32),
        ],
        axis=0,
    )
    left, y_hat, z_hat = hats_of(record, rotations, ligand_coords, atom_types, channel_weights)
    turned = turned_product(folded, left, y_hat, z_hat, width).reshape(1, 2, GRID, width)
    index = jnp.arange(GRID, dtype=jnp.int32)
    halves = lax.all_to_all(turned, "fft", split_axis=2, concat_axis=3, tiled=True)
    volume = halves.reshape(2, slab, GRID, GRID)
    cosine, sine = waves(index, index)
    z_turn = jnp.stack([cosine, -sine])

    def scores(places):
        y_cos, y_sin = waves(index, places)
        y_turn = jnp.stack([jnp.stack([y_cos, -y_sin]), jnp.stack([y_sin, y_cos])])
        in_y = jnp.einsum("dcky,cxkz->dxyz", y_turn, volume, precision=HIGH)
        part = jnp.einsum("dxyz,dzt->xyt", in_y, z_turn, precision=HIGH)
        return part.reshape(1, slab, places.shape[0] * GRID)

    count = lax.axis_size("chan")
    if count != 2:
        return lax.psum_scatter(scores(index), "chan", scatter_dimension=2, tiled=True)
    near = lax.axis_index("chan") * HALF + jnp.arange(HALF, dtype=jnp.int32)
    far = (near + HALF) % GRID
    arrived = from_behind(scores(far), "chan", 1)
    return scores(near) + arrived


def solution(mesh):
    in_specs = (
        P(("grp", "rec")),
        P(),
        P(None, "grp"),
        P("grp"),
        P(None, "chan"),
        P("rec", "chan", None, None, "fft"),
    )
    out_specs = P(("grp", "rec"), "fft", "chan")
    return jax.shard_map(body, mesh=mesh, in_specs=in_specs, out_specs=out_specs, check_vma=False)
```

time: 81.2 us -> 81.8 us (level)
  matrix products: 26.1 us -> 4.09 us
  Pallas kernels: 0 us -> 21.7 us
  local copies, waits for them, and re-layouts: 10.7 us -> 28 us
  waiting for transfers between devices: 21.9 us -> 5.47 us
  starting transfers between devices: 7.82 us -> 5.74 us
  other arithmetic: 9.42 us -> 11.4 us
    dot_general x13 -> x3, matrix products: 23.5 us -> 1.52 us  [the longest x1 0.8 us: hats_of(): jnp.dot(picks, rotations.reshape(table_rows, 9), precision=HIGHEST)[0]]
    pallas_call x0 -> x1, Pallas kernels: none -> 21.7 us  [turned_product(): pl.pallas_call(functools.partial(window_kernel, lax.axis_size('rec')), ou...]
    ppermute x4 -> x2, waiting for transfers between devices: 21.9 us -> 5.47 us  [from_behind(): return lax.ppermute(value, axis, pairs)]
    unnamed x14 -> x31, local copies, waits for them, and re-layouts: 3.04 us -> 18.8 us
    slice x3, local copies, waits for them, and re-layouts: 0.29 us -> 2.72 us  [fold(): jnp.roll(back, 1, axis=2)]
    ppermute x4 -> x2, starting transfers between devices: 7.31 us -> 5.21 us  [from_behind(): return lax.ppermute(value, axis, pairs)]
    mul x1, other arithmetic: 0.35 us -> 1.89 us  [fold(): inner = mirrored[:, :HALF - 1] * sign]
    another operation x2, other arithmetic: 0.02 us -> 1.27 us  [scores(): y_turn = jnp.stack([jnp.stack([y_cos, -y_sin]), jnp.stack([y_sin, y_cos])])]
  transfers between devices with their start and end apart: 5 -> 3, of which waited for: 3 -> 1; matrix products, arithmetic and copies ran while one was open for 26% -> 15% of each run, Pallas kernels for 0% -> 0%
where the time goes in v3:
time: 81.8 us; the launch traced here: 81.3 us
  local copies, waits for them, and re-layouts  28 us (34%)
  Pallas kernels  21.7 us (27%)
  other arithmetic  11.4 us (14%)
  starting transfers between devices  5.74 us (7%)
  waiting for transfers between devices  5.47 us (7%)
  blocking collectives  4.58 us (6%)
  matrix products  4.09 us (5%)
    pallas_call x1, Pallas kernels, turned_product(): pl.pallas_call(functools.partial(window_kernel, lax.axis_size('rec')), ou...  21.7 us
    unnamed x31, local copies, waits for them, and re-layouts  18.8 us
    add x1, other arithmetic, hats_of(): 0.5 * GRID  5.67 us
    ppermute x2, waiting for transfers between devices, from_behind(): return lax.ppermute(value, axis, pairs)  5.47 us
    ppermute x2, starting transfers between devices, from_behind(): return lax.ppermute(value, axis, pairs)  5.21 us
    all_to_all x1, blocking collectives, body(): lax.all_to_all(turned, 'fft', split_axis=2, concat_axis=3, tiled=True)  4.58 us
    slice x3, local copies, waits for them, and re-layouts, fold(): jnp.roll(back, 1, axis=2)  2.72 us
    mul x1, other arithmetic, fold(): inner = mirrored[:, :HALF - 1] * sign  1.89 us
  transfers between devices with their start and end apart: 3, of which 1 were waited for; matrix products, arithmetic and copies ran while one was open for 15% of the time, Pallas kernels for 0%

profile of v3, /device:TPU:0, one launch (start us, length us, event | category | flops | bytes accessed | tf_op | source)
XLA Modules:
  0.0 81.3 jit_solution(15960316809427685654)
XLA Ops:
  0.0 0.0 copy-start
  0.0 0.0 copy-start.12
  0.0 2.1 %copy.55 = f32[1,1,2,64,2048]{4,2,3,1,0:T(2,128)S(1)} copy(f32[1,1,2,64,2048]{4,3,2,1,0:T(8,128)} %param.16) | data formatting | bytes 2097152 | tf_op args[5]
  2.1 0.5 collective-permute-start
  2.7 3.7 %collective-permute-start.1 = (s32[1]{0:T(128)}, s32[1]{0:T(128)}, u32[]{:S(2)}, u32[]{:S(2)}) collective-permute-start(s32[1]{0:T(128)} %param.11), channel_id=1, source_target_pairs={{0,8},{4,12},{8,0},{12,4},{1,9},{5,13},{9,1},{13,5},{2,10},{6,14},... | collective-permute-start | bytes 20 | tf_op jit(solution)/shard_map/ppermute | solution.py:22
  6.3 0.1 sine_negate_fusion
  6.5 0.2 fusion.56
  6.7 0.0 copy-done.10
  6.7 0.2 fusion.57
  6.9 0.1 pad.27.clone
  7.0 0.0 copy-done.12
  7.0 0.3 fusion.14
  7.3 0.6 maximum_bitcast_fusion.7
  7.9 0.6 maximum_bitcast_fusion.9
  8.6 0.0 collective-permute-done.1
  8.6 0.8 convolution_bitcast_fusion.2
  9.4 0.7 fusion.73
  10.1 5.7 %add_add_fusion = (f32[1,512]{1,0:T(1,128)S(1)}, f32[1,512]{1,0:T(1,128)S(1)}, f32[1,512]{1,0:T(1,128)S(1)}) fusion(f32[]{:T(128)} %bitcast.19, f32[]{:T(128)} %bitcast.18, f32[]{:T(128)} %bitcast.17, f32[3,512]{1,0:T(4,128)S(1)} %convert_multiply_fusion, f32[]{:T(128)} %bitcast.9, f32[]{:T(128)} %bitcast.8, f32[]{:T(128)} %bitcast.7, f32[]{:T(128)} %bitcast.13, ...), kind=kLoop, calls=%fused_computation.98 | loop fusion | flops 9216 | bytes 12324 | tf_op jit(solution)/shard_map/add | solution.py:236
  15.7 0.0 copy-done.8
  15.8 0.4 fusion.16
  16.2 0.1 reshape.470.l_ref
  16.3 0.1 fusion.13
  16.4 0.2 fusion.12
  16.6 0.3 pad_maximum_fusion.2
  16.9 0.0 collective-permute-done
  16.9 0.3 broadcast_select_fusion
  17.2 0.6 slice.114
  17.8 0.6 slice.113
  18.5 0.6 slice.116
  19.1 0.0 copy-start.11
  19.1 6.5 %reverse.4 = f32[2,32,2048]{2,0,1:T(2,128)} reverse(f32[2,32,2048]{2,0,1:T(2,128)S(1)} %bitcast.88), dimensions={1,2} | reverse | bytes 1048576
  25.6 1.6 %slice.134 = f32[2,32,2047]{2,0,1:T(2,128)S(1)} slice(f32[2,32,2048]{2,0,1:T(2,128)} %reverse.4), slice={[0:2], [0:32], [1:2048]} | slice | bytes 1048064
  27.3 1.5 %slice.89 = f32[2,32,1]{2,0,1:T(2,128)} reverse(f32[2,32,1]{2,0,1:T(2,128)} %slice.113), dimensions={1,2} | reverse | bytes 512 | tf_op jit(solution)/shard_map/jit(_roll_static)/slice | solution.py:41
  28.7 6.3 %reverse.5 = f32[2,32,2048]{2,0,1:T(2,128)} reverse(f32[2,32,2048]{2,0,1:T(2,128)S(1)} %bitcast.87), dimensions={1,2} | reverse | bytes 1048576
  35.1 1.6 %slice.135 = f32[2,32,1983]{2,0,1:T(2,128)S(1)} slice(f32[2,32,2048]{2,0,1:T(2,128)} %reverse.5), slice={[0:2], [0:32], [65:2048]} | slice | bytes 1015296
  36.7 0.7 slice.93
  37.5 0.0 copy-done.11
  37.5 1.9 %fusion.11 = f32[2,31,2048]{2,0,1:T(2,128)S(1)} fusion(f32[2,32,2047]{2,0,1:T(2,128)S(1)} %slice.134, f32[2,32,1]{2,0,1:T(2,128)} %slice.89, f32[2,32,1983]{2,0,1:T(2,128)S(1)} %slice.135, f32[2,32,65]{2,0,1:T(2,128)} %slice.93, pred[2048]{0:T(1024)(128)(4,1)S(1)} %fusion.48, f32[2]{0:T(128)S(1)} %copy-done.11), kind=kLoop, calls=%fused_computation.15 | loop fusion | flops 507904 | bytes 1558536 | tf_op jit(solution)/shard_map/mul | solution.py:43
  39.4 0.0 copy-start.1
  39.4 0.0 copy-start.2
  39.4 0.0 copy-start.3
  39.4 0.3 slice_add_fusion
  39.7 0.3 copy.28
  40.1 0.1 maximum_maximum_fusion.g_ref
  40.2 0.6 copy-done.1
  40.8 0.0 copy-done.2
  40.8 21.7 %shard_map.109 = f32[128,2048]{1,0:T(8,128)S(1)} custom-call(f32[72,2048]{1,0:T(8,128)S(1)} %maximum_maximum_fusion.g_ref, f32[72,1024]{1,0:T(8,128)S(1)} %reshape.470.l_ref, bf16[512,192]{1,0:T(8,128)(2,1)S(1)} %get-tuple-element.31.y_ref, bf16[512,192]{1,0:T(8,128)(2,1)S(1)} %get-tuple-element.32.z_ref, bf16[8,192,512]{2,1,0:T(8,128)(2,1)S(1)} %copy-done.1, ...), custom_call_target="tpu_custom_call" | custom-call | tf_op jit(solution)/shard_map/pallas_call | solution.py:197
  62.5 0.8 copy.31
  63.3 4.6 %all_to_all.15 = f32[1,2,64,2048]{3,1,0,2:T(2,128)S(1)} all-to-all(f32[1,2,64,2048]{3,1,0,2:T(2,128)S(1)} %copy.31), channel_id=1, replica_groups=mesh['grp'=2,'rec'=4,'chan'=2,'fft'=2] {'fft'}, dimensions={2} | all-to-all | bytes 2097152 | tf_op jit(solution)/shard_map/all_to_all | solution.py:274
  67.9 0.6 copy.32
  68.5 0.8 copy.33
  69.3 0.0 copy-start.6
  69.4 0.0 copy-start.7
  69.4 1.2 %reshape.473 = f32[2,32,64,64]{3,2,1,0:T(8,128)S(1)} reshape(f32[1,2,32,2,2048]{4,3,2,1,0:T(2,128)S(1)} %copy.33) | data formatting | bytes 2097152 | tf_op jit(solution)/shard_map/reshape | solution.py:275
  70.6 0.0 copy-start.5
  70.6 0.7 fusion.7
  71.3 0.6 convolution_bitcast_fusion
  71.9 0.2 reshape.475
  72.1 1.6 %collective-permute-start.2 = (f32[1,32,2048]{2,1,0:T(8,128)S(1)}, f32[1,32,2048]{2,1,0:T(8,128)S(1)}, u32[]{:S(2)}, u32[]{:S(2)}) collective-permute-start(f32[1,32,2048]{2,1,0:T(8,128)S(1)} %reshape.475), channel_id=1, source_target_pairs={{0,2},{2,0},{1,3},{3,1},{4,6},{6,4},{5,7},{7,5},{8,10},{10,8},{9,1... | collective-permute-start | bytes 786440 | tf_op jit(solution)/shard_map/ppermute | solution.py:22
  73.6 0.7 fusion.4
  74.3 0.6 convolution_bitcast_fusion.1
  74.9 0.2 reshape.474
  75.1 5.5 %collective-permute-done.2 = f32[1,32,2048]{2,1,0:T(8,128)S(1)} collective-permute-done((f32[1,32,2048]{2,1,0:T(8,128)S(1)}, f32[1,32,2048]{2,1,0:T(8,128)S(1)}, u32[]{:S(2)}, u32[]{:S(2)}) %collective-permute-start.2) | collective-permute-done | bytes 262176 | tf_op jit(solution)/shard_map/ppermute | solution.py:22
  80.6 0.7 add.202
  (23 shorter events, 0.2 us)
Async XLA Ops:
  0.0 7.0 %copy-start = (f32[18,1]{0,1:T(1,128)S(1)}, f32[18,1]{0,1:T(1,128)}, u32[]{:S(2)}) copy-start(f32[18,1]{0,1:T(1,128)} %param.15) | copy-start | bytes 220
  0.0 15.7 %copy-start.8 = (f32[144,64]{1,0:T(8,128)S(1)}, f32[144,64]{1,0:T(8,128)}, u32[]{:S(2)}) copy-start(f32[144,64]{1,0:T(8,128)} %constant.100.clone) | copy-start | bytes 110596
  0.0 6.7 %copy-start.10 = (f32[64,3,3]{0,2,1:T(4,128)S(1)}, f32[64,3,3]{0,2,1:T(4,128)}, u32[]{:S(2)}) copy-start(f32[64,3,3]{0,2,1:T(4,128)} %param.12) | copy-start | bytes 6916
  0.0 6.7 %copy-start.9 = (s32[3,512]{1,0:T(4,128)S(1)}, s32[3,512]{1,0:T(4,128)}, u32[]{:S(2)}) copy-start(s32[3,512]{1,0:T(4,128)} %param.13) | copy-start | bytes 18436
  0.0 7.0 %copy-start.12 = (s32[512]{0:T(512)S(1)}, s32[512]{0:T(512)}, u32[]{:S(2)}) copy-start(s32[512]{0:T(512)} %param.14) | copy-start | bytes 6148
  2.1 14.8 %collective-permute-start = (f32[2,32,2048]{2,0,1:T(2,128)S(1)}, f32[2,32,2048]{2,0,1:T(2,128)S(1)}, u32[]{:S(2)}, u32[]{:S(2)}) collective-permute-start(f32[2,32,2048]{2,0,1:T(2,128)S(1)} %slice.112), channel_id=1, source_target_pairs={{0,1},{1,0},{2,3},{3,2},{4,5},{5,4},{6,7},{7,6},{8,9},{9,8},{10,11... | collective-permute-start | bytes 1572872 | tf_op jit(solution)/shard_map/ppermute | solution.py:38
  2.7 5.9 %collective-permute-start.1 = (s32[1]{0:T(128)}, s32[1]{0:T(128)}, u32[]{:S(2)}, u32[]{:S(2)}) collective-permute-start(s32[1]{0:T(128)} %param.11), channel_id=1, source_target_pairs={{0,8},{4,12},{8,0},{12,4},{1,9},{5,13},{9,1},{13,5},{2,10},{6,14},... | collective-permute-start | bytes 20 | tf_op jit(solution)/shard_map/ppermute | solution.py:22
  17.2 10.0 %copy-start.4 = (f32[2,32,2048]{2,0,1:T(2,128)}, f32[2,32,2048]{2,0,1:T(2,128)S(1)}, u32[]{:S(2)}) copy-start(f32[2,32,2048]{2,0,1:T(2,128)S(1)} %broadcast_select_fusion) | copy-start | bytes 1572868
  19.1 18.4 %copy-start.11 = (f32[2]{0:T(128)S(1)}, f32[2]{0:T(128)}, u32[]{:S(2)}) copy-start(f32[2]{0:T(128)} %constant.99.clone) | copy-start | bytes 28
  28.7 8.0 %slice-start = ((f32[2,32,2048]{2,0,1:T(2,128)}), f32[2,32,65]{2,0,1:T(2,128)S(1)}, s32[]{:S(2)}) async-start(f32[2,32,2048]{2,0,1:T(2,128)} %copy-done.4), calls=%async_computation.1 | async-start | bytes 65536 | tf_op jit(solution)/shard_map/jit(_roll_static)/slice | solution.py:41
  39.4 1.4 %copy-start.1 = (bf16[8,192,512]{2,1,0:T(8,128)(2,1)S(1)}, bf16[8,192,512]{2,1,0:T(8,128)(2,1)}, u32[]{:S(2)}) copy-start(bf16[8,192,512]{2,1,0:T(8,128)(2,1)} %constant.101.clone.yt_ref) | copy-start | bytes 4718596
  39.4 1.4 %copy-start.2 = (bf16[192,512]{1,0:T(8,128)(2,1)S(1)}, bf16[192,512]{1,0:T(8,128)(2,1)}, u32[]{:S(2)}) copy-start(bf16[192,512]{1,0:T(8,128)(2,1)} %constant.102.clone.zt_ref) | copy-start | bytes 589828
  39.4 1.4 %copy-start.3 = (f32[128,72]{1,0:T(8,128)S(1)}, f32[128,72]{1,0:T(8,128)}, u32[]{:S(2)}) copy-start(f32[128,72]{1,0:T(8,128)} %constant.103.clone.turn_ref) | copy-start | bytes 110596
  69.3 1.2 %copy-start.6 = (f32[1,2,64,32]{2,3,1,0:T(8,128)S(1)}, f32[1,2,64,32]{2,3,1,0:T(8,128)}, u32[]{:S(2)}) copy-start(f32[1,2,64,32]{2,3,1,0:T(8,128)} %get-tuple-element.5) | copy-start | bytes 49156
  69.4 1.2 %copy-start.7 = (f32[1,2,64,32]{2,3,1,0:T(8,128)S(1)}, f32[1,2,64,32]{2,3,1,0:T(8,128)}, u32[]{:S(2)}) copy-start(f32[1,2,64,32]{2,3,1,0:T(8,128)} %get-tuple-element.6) | copy-start | bytes 49156
  70.6 3.0 %copy-start.5 = (f32[1,2,64,32]{2,3,1,0:T(8,128)S(1)}, f32[1,2,64,32]{2,3,1,0:T(8,128)}, u32[]{:S(2)}) copy-start(f32[1,2,64,32]{2,3,1,0:T(8,128)} %get-tuple-element.8) | copy-start | bytes 49156
  72.1 8.5 %collective-permute-start.2 = (f32[1,32,2048]{2,1,0:T(8,128)S(1)}, f32[1,32,2048]{2,1,0:T(8,128)S(1)}, u32[]{:S(2)}, u32[]{:S(2)}) collective-permute-start(f32[1,32,2048]{2,1,0:T(8,128)S(1)} %reshape.475), channel_id=1, source_target_pairs={{0,2},{2,0},{1,3},{3,1},{4,6},{6,4},{5,7},{7,5},{8,10},{10,8},{9,1... | collective-permute-start | bytes 786440 | tf_op jit(solution)/shard_map/ppermute | solution.py:22

commit v4 on v3

--- a/solution.py
+++ b/solution.py
@@ -28,23 +28,6 @@
     return jnp.cos(angle), jnp.sin(angle)
 
 
-def hat_rows(places, cells):
-    return jnp.maximum(0.0, 1.0 - jnp.abs(places[:, None] - cells[None, :]))
-
-
-def fold(receptor, width):
-    lane = jnp.arange(width, dtype=jnp.int32)
-    upper = receptor[:, HALF:]
-    other = lax.ppermute(upper, "fft", [(0, 1), (1, 0)])
-    source = jnp.where(lane < GRID, upper, other)
-    back = lax.rev(source, (1, 2))
-    mirrored = jnp.where(lane % GRID == 0, jnp.roll(back, 1, axis=2), jnp.roll(back, 65, axis=2))
-    sign = jnp.array([1.0, -1.0], jnp.float32)[:, None, None]
-    inner = mirrored[:, : HALF - 1] * sign
-    inner = jnp.pad(inner, ((0, 0), (1, 1), (0, 0)))
-    return receptor[:, : HALF + 1] + inner
-
-
 def host_waves(rows, columns):
     angle = (np.outer(rows, columns) % GRID) * (2.0 * np.pi / GRID)
     return np.cos(angle), np.sin(angle)
@@ -71,24 +54,26 @@
 
 
 def window_kernel(
-    count, g_ref, l_ref, y_ref, z_ref, yt_ref, zt_ref, turn_ref, out_ref,
-    own, first, pair, second, win, lig, z_wave, l_high, l_low,
-    send1, recv1, send2, recv2, send3, recv3,
+    count, s_ref, flip_ref, rows_ref, l_ref, y_ref, z_ref, yt_ref, zt_ref, turn_ref, out_ref,
+    source, own, first, pair, second, win, lig, z_wave, l_high, l_low,
+    send0, recv0, send1, recv1, send2, recv2, send3, recv3,
 ):
     grp = lax.axis_index("grp")
     rec = lax.axis_index("rec")
     after = lax.rem(rec + 1, count)
     before = lax.rem(rec + count - 1, count)
-    chunks = own.shape[0]
+    chunks = win.shape[0]
     mine = chunks // 2
     barrier = pltpu.get_barrier_semaphore()
-    for target in ({"rec": after}, {"rec": before}, {"grp": 1 - grp}):
+    fft = lax.axis_index("fft")
+    for target in ({"rec": after}, {"rec": before}, {"grp": 1 - grp}, {"fft": 1 - fft}):
         pl.semaphore_signal(
             barrier, inc=1, device_id=target, device_id_type=pl.DeviceIdType.MESH
         )
-    for chunk in range(chunks):
-        own[chunk] = g_ref[:, chunk * LANES : (chunk + 1) * LANES]
-    pl.semaphore_wait(barrier, 3)
+    width = s_ref.shape[2]
+    for part in range(2):
+        source[part * HALF : (part + 1) * HALF, width:] = s_ref[part, HALF:, 0:128]
+    pl.semaphore_wait(barrier, 4)
     base = grp * mine
 
     def remote(source, target, send, recv, device):
@@ -98,7 +83,7 @@
         )
 
     ones = [
-        remote(own.at[base + c], first.at[c], send1.at[c], recv1.at[c], {"rec": after})
+        remote(own.at[c], first.at[c], send1.at[c], recv1.at[c], {"rec": after})
         for c in range(mine)
     ]
     twos = [
@@ -109,13 +94,35 @@
         remote(win.at[base + c], win.at[base + c], send3.at[c], recv3.at[c], {"grp": 1 - grp})
         for c in range(mine)
     ]
-    for copy in ones:
+    reach = pl.ds(pl.multiple_of((1 - grp) * (width // 2 - 128), 128), width // 2 + 128)
+    zeros = [
+        remote(
+            s_ref.at[part, pl.ds(HALF, HALF), reach],
+            source.at[pl.ds(part * HALF, HALF), reach],
+            send0.at[part], recv0.at[part], {"fft": 1 - fft},
+        )
+        for part in range(2)
+    ]
+    for copy in zeros:
         copy.start()
 
     z_wave[...] = dot(z_ref[...], zt_ref[...])
     high, low = split(l_ref[...])
     l_high[...] = high
     l_low[...] = low
+
+    def fold(c):
+        chunk = base + c
+        window = pl.ds(pl.multiple_of((2 * (chunks - 1) - 2 * chunk) * 128, 128), 384)
+        high, low = split(source[:, window])
+        flipped = dot(jnp.concatenate([high, low], axis=0), flip_ref[...])
+        mirrored = dot(rows_ref[...], flipped.astype(jnp.bfloat16))
+        lanes = pl.ds(pl.multiple_of(chunk * LANES, LANES), LANES)
+        own[c, 0:32] = s_ref[0, 0:32, lanes] + mirrored[0:32]
+        own[c, 32:64] = s_ref[1, 0:32, lanes] + mirrored[32:64]
+        row = lax.broadcasted_iota(jnp.int32, (8, LANES), 0)
+        re, im = s_ref[0, 32:40, lanes][0:1], s_ref[1, 32:40, lanes][0:1]
+        own[c, 64:72] = jnp.where(row == 0, re, jnp.where(row == 1, im, 0.0))
 
     def ligand(chunk):
         y_wave = dot(y_ref[...], yt_ref[chunk])
@@ -145,27 +152,32 @@
         out_ref[:, lanes] = dot(t_high, p_high) + dot(t_low, p_high) + dot(t_high, p_low)
 
     ligand(0)
+    for copy in zeros:
+        copy.wait_recv()
+    for c in range(mine):
+        fold(c)
+        ones[c].start()
     ligand(1)
     ligand(2)
     for c in range(mine):
         ones[c].wait_recv()
-        pair[c] = own[base + c] + first[c]
+        pair[c] = own[c] + first[c]
         twos[c].start()
         ligand(3 + c)
     ligand(7)
     for c in range(mine):
         twos[c].wait_recv()
-        win[base + c] = own[base + c] + second[c]
+        win[base + c] = own[c] + second[c]
         threes[c].start()
         product(base + c)
     for c in range(mine):
         threes[c].wait_recv()
         product((1 - grp) * mine + c)
-    for copy in ones + twos + threes:
+    for copy in zeros + ones + twos + threes:
         copy.wait_send()
 
 
-def turned_product(folded, left, y_hat, z_hat, width):
+def turned_product(receptor, left, y_hat, z_hat, width):
     index = np.arange(GRID)
     chunks = width // LANES
     lane = np.arange(width)
@@ -191,16 +203,27 @@
         high = lax.reduce_precision(value, 8, 7)
         return jnp.concatenate([high, value - high, high], axis=1).astype(jnp.bfloat16)
 
+    flip = np.zeros((384, LANES), np.float32)
+    for m in range(LANES // GRID):
+        for kz in range(GRID):
+            flip[(4 - m) * GRID + (-kz) % GRID, m * GRID + kz] = 1.0
+    flip = flip.astype(jnp.bfloat16)
+    rows = np.zeros((2 * HALF, 2 * HALF), np.float32)
+    for kx in range(1, HALF):
+        rows[kx, HALF - kx] = 1.0
+        rows[HALF + kx, 2 * HALF - kx] = -1.0
+    rows = np.concatenate([rows, rows], axis=1).astype(jnp.bfloat16)
     atoms = y_hat.shape[0]
     piece = (ROWS, LANES)
     half = chunks // 2
     return pl.pallas_call(
         functools.partial(window_kernel, lax.axis_size("rec")),
         out_shape=jax.ShapeDtypeStruct((2 * GRID, width), jnp.float32),
-        in_specs=[pl.BlockSpec(memory_space=pltpu.VMEM)] * 7,
+        in_specs=[pl.BlockSpec(memory_space=pltpu.VMEM)] * 9,
         out_specs=pl.BlockSpec(memory_space=pltpu.VMEM),
         scratch_shapes=[
-            pltpu.VMEM((chunks,) + piece, jnp.float32),
+            pltpu.VMEM((2 * HALF, width + 128), jnp.float32),
+            pltpu.VMEM((half,) + piece, jnp.float32),
             pltpu.VMEM((half,) + piece, jnp.float32),
             pltpu.VMEM((half,) + piece, jnp.float32),
             pltpu.VMEM((half,) + piece, jnp.float32),
@@ -210,12 +233,13 @@
             pltpu.VMEM((ROWS, 2 * atoms), jnp.bfloat16),
             pltpu.VMEM((ROWS, 2 * atoms), jnp.bfloat16),
         ]
+        + [pltpu.SemaphoreType.DMA((2,))] * 2
         + [pltpu.SemaphoreType.DMA((half,))] * 6,
         compiler_params=pltpu.CompilerParams(
             collective_id=0, has_side_effects=True, vmem_limit_bytes=40 * 1024 * 1024
         ),
     )(
-        folded, left, columns(y_hat), columns(z_hat),
+        receptor, jnp.asarray(flip), jnp.asarray(rows), left, columns(y_hat), columns(z_hat),
         jnp.asarray(y_table), jnp.asarray(z_table), jnp.asarray(turn),
     )
 
@@ -230,27 +254,28 @@
     type_hot = (atom_types[:, None] == jnp.arange(kinds, dtype=jnp.int32)[None, :]).astype(
         jnp.float32
     )
-    weights = jnp.dot(type_hot, channel_weights, precision=HIGHEST)
+    weights = jnp.dot(
+        type_hot, jnp.broadcast_to(channel_weights, (kinds, GRID)), precision=HIGHEST
+    )
     coords = ligand_coords.astype(jnp.float32) * (1.0 / 256.0)
-    places = [
-        0.5 * GRID
-        + (
-            matrix[3 * row] * coords[0]
-            + matrix[3 * row + 1] * coords[1]
-            + matrix[3 * row + 2] * coords[2]
-        )
-        for row in range(3)
-    ]
+    matrix = matrix.reshape(3, 3)
+    center = 0.5 * GRID
     cells = jnp.arange(GRID, dtype=jnp.float32)
+    offset = center - jnp.concatenate([cells, cells])
+    spread = jnp.repeat(matrix[1:].T, GRID, axis=1)
+    hats = jnp.maximum(
+        0.0, 1.0 - jnp.abs(jnp.dot(coords.T, spread, precision=HIGHEST) + offset[None, :])
+    )
+    x_places = jnp.dot(jnp.broadcast_to(matrix[0], (GRID, 3)), coords, precision=HIGHEST)
+    x_hat = jnp.maximum(0.0, 1.0 - jnp.abs(x_places + (center - cells)[:, None]))
     odd = (jnp.arange(GRID, dtype=jnp.int32) * lax.axis_index("fft")) % 2
-    y_hat = hat_rows(places[1], cells) * weights * (1.0 - 2.0 * odd.astype(jnp.float32))
-    z_hat = hat_rows(places[2], cells)
+    y_hat = hats[:, :GRID] * weights * (1.0 - 2.0 * odd.astype(jnp.float32))
+    z_hat = hats[:, GRID:]
     cosine, sine = host_waves(np.arange(HALF + 1), np.arange(GRID))
     none = np.zeros((6, GRID))
     meet_re = np.concatenate([cosine[:HALF], sine[:HALF], cosine[HALF:], sine[HALF:], none], 0)
     meet_im = np.concatenate([-sine[:HALF], cosine[:HALF], -sine[HALF:], cosine[HALF:], none], 0)
     table = jnp.asarray(np.stack([meet_re, meet_im], axis=1).reshape(2 * ROWS, GRID), jnp.float32)
-    x_hat = jnp.maximum(0.0, 1.0 - jnp.abs(places[0][None, :] - cells[:, None]))
     left = jnp.dot(table, x_hat, precision=HIGHEST).reshape(ROWS, 2 * x_hat.shape[1])
     return left, y_hat, z_hat
 
@@ -259,17 +284,8 @@
     width = receptor_spectra.shape[-1]
     slab = GRID // lax.axis_size("fft")
     record = from_behind(record_ids, "rec", 2)
-    folded = fold(receptor_spectra[0, 0], width)
-    folded = jnp.concatenate(
-        [
-            folded[:, :HALF].reshape(GRID, width),
-            folded[:, HALF],
-            jnp.zeros((ROWS - GRID - 2, width), jnp.float32),
-        ],
-        axis=0,
-    )
     left, y_hat, z_hat = hats_of(record, rotations, ligand_coords, atom_types, channel_weights)
-    turned = turned_product(folded, left, y_hat, z_hat, width).reshape(1, 2, GRID, width)
+    turned = turned_product(receptor_spectra[0, 0], left, y_hat, z_hat, width).reshape(1, 2, GRID, width)
     index = jnp.arange(GRID, dtype=jnp.int32)
     halves = lax.all_to_all(turned, "fft", split_axis=2, concat_axis=3, tiled=True)
     volume = halves.reshape(2, slab, GRID, GRID)

time: 81.8 us -> 60.4 us (0.74)
  local copies, waits for them, and re-layouts: 28 us -> 6.06 us
  other arithmetic: 11.4 us -> 5.2 us
  matrix products: 4.09 us -> 8.89 us
  Pallas kernels: 21.7 us -> 23.8 us
    unnamed x31 -> x30, local copies, waits for them, and re-layouts: 18.8 us -> 0.1 us
    add x2 -> x0, other arithmetic: 5.95 us -> none  [the longest x1 5.67 us: hats_of(): 0.5 * GRID]
    slice x11 -> x2, local copies, waits for them, and re-layouts: 5.16 us -> 0.16 us  [hats_of(): spread = jnp.repeat(matrix[1:].T, GRID, axis=1)]
    dot_general x1 -> x3, matrix products: 0.31 us -> 3.55 us  [the longest x1 1.31 us: hats_of(): jnp.dot(coords.T, spread, precision=HIGHEST) + offset[None, :]]
    pallas_call x1, Pallas kernels: 21.7 us -> 23.8 us  [turned_product(): pl.pallas_call(functools.partial(window_kernel, lax.axis_size('rec')), ou...]
    mul x2 -> x0, other arithmetic: 1.9 us -> none  [the longest x1 1.89 us: fold(): inner = mirrored[:, :HALF - 1] * sign]
    dot_general x1, matrix products: 0.41 us -> 1.97 us  [hats_of(): jnp.dot(table, x_hat, precision=HIGHEST).reshape(ROWS, 2 * x_hat.shape[1])]
    concatenate x1, other arithmetic: 0.27 us -> 1.23 us  [columns(): jnp.concatenate([high, value - high, high], axis=1).astype(jnp.bfloat16)]
  transfers between devices with their start and end apart: 3 -> 2, of which waited for: 1 -> 1; matrix products, arithmetic and copies ran while one was open for 15% -> 8% of each run, Pallas kernels for 0% -> 0%
where the time goes in v4:
time: 60.4 us; the launch traced here: 59.9 us
  Pallas kernels  23.8 us (39%)
  matrix products  8.89 us (15%)
  local copies, waits for them, and re-layouts  6.06 us (10%)
  starting transfers between devices  5.66 us (9%)
  waiting for transfers between devices  5.43 us (9%)
  other arithmetic  5.2 us (9%)
  blocking collectives  4.58 us (8%)
    pallas_call x1, Pallas kernels, turned_product(): pl.pallas_call(functools.partial(window_kernel, lax.axis_size('rec')), ou...  23.8 us
    ppermute x2, starting transfers between devices, from_behind(): return lax.ppermute(value, axis, pairs)  5.66 us
    ppermute x2, waiting for transfers between devices, from_behind(): return lax.ppermute(value, axis, pairs)  5.43 us
    all_to_all x1, blocking collectives, body(): lax.all_to_all(turned, 'fft', split_axis=2, concat_axis=3, tiled=True)  4.58 us
    dot_general x1, matrix products, hats_of(): jnp.dot(table, x_hat, precision=HIGHEST).reshape(ROWS, 2 * x_hat.shape[1])  1.97 us
    all_to_all x2, local copies, waits for them, and re-layouts, body(): lax.all_to_all(turned, 'fft', split_axis=2, concat_axis=3, tiled=True)  1.42 us
    dot_general x2, matrix products, scores(): in_y = jnp.einsum('dcky,cxkz->dxyz', y_turn, volume, precision=HIGH)  1.38 us
    dot_general x1, matrix products, hats_of(): jnp.dot(coords.T, spread, precision=HIGHEST) + offset[None, :]  1.31 us
  transfers between devices with their start and end apart: 2, of which 1 were waited for; matrix products, arithmetic and copies ran while one was open for 8% of the time, Pallas kernels for 0%

profile of v4, /device:TPU:0, one launch (start us, length us, event | category | flops | bytes accessed | tf_op | source)
XLA Modules:
  0.0 59.9 jit_solution(14682863328788401826)
XLA Ops:
  0.0 0.0 copy-start
  0.0 0.0 copy-start.3
  0.0 0.0 copy-start.6
  0.0 0.0 copy-start.4
  0.0 0.0 copy-start.5
  0.0 0.0 copy-start.14
  0.0 0.0 copy-start.2
  0.1 4.1 %collective-permute-start = (s32[1]{0:T(128)}, s32[1]{0:T(128)}, u32[]{:S(2)}, u32[]{:S(2)}) collective-permute-start(s32[1]{0:T(128)} %param.12), channel_id=1, source_target_pairs={{0,8},{4,12},{8,0},{12,4},{1,9},{5,13},{9,1},{13,5},{2,10},{6,14},... | collective-permute-start | bytes 20 | tf_op jit(solution)/shard_map/ppermute | solution.py:22
  4.2 0.8 %sine_negate_fusion = (f32[1,64,64]{2,1,0:T(8,128)}, f32[1,64,64]{2,1,0:T(8,128)}) fusion(), kind=kLoop, calls=%fused_computation.46 | loop fusion | flops 61440 | bytes 32768 | tf_op jit(solution)/shard_map/neg | solution.py:293
  5.0 0.7 %reshape.428 = f32[64,9]{0,1:T(8,128)S(1)} reshape(f32[64,3,3]{0,2,1:T(4,128)} %param.13) | data formatting | bytes 4608 | tf_op jit(solution)/shard_map/reshape | solution.py:252
  5.7 0.1 maximum_subtract_fusion
  5.8 0.2 fusion.50
  5.9 0.2 fusion.49
  6.1 0.6 %maximum_bitcast_fusion.9 = (f32[1,2,64,32]{2,3,1,0:T(8,128)}, f32[1,2,64,32]{2,3,1,0:T(8,128)}) fusion(f32[1,64,32]{1,2,0:T(8,128)S(1)} %get-tuple-element.13, f32[1,64,32]{1,2,0:T(8,128)S(1)} %get-tuple-element.15, f32[1,64,32]{1,2,0:T(8,128)S(1)} %get-tuple-element.14), kind=kLoop, calls=%fused_computation.44 | loop fusion | flops 8192 | bytes 57344 | tf_op jit(solution)/shard_map/stack | solution.py:297
  6.7 0.6 %maximum_bitcast_fusion.7 = (f32[1,2,64,32]{2,3,1,0:T(8,128)}, f32[1,2,64,32]{2,3,1,0:T(8,128)}) fusion(f32[1,64,32]{1,2,0:T(8,128)S(1)} %get-tuple-element.16, f32[1,64,32]{1,2,0:T(8,128)S(1)} %get-tuple-element.18, f32[1,64,32]{1,2,0:T(8,128)S(1)} %get-tuple-element.17), kind=kLoop, calls=%fused_computation.42 | loop fusion | flops 8192 | bytes 57344 | tf_op jit(solution)/shard_map/stack | solution.py:297
  7.4 0.0 collective-permute-done
  7.4 0.8 %convolution_bitcast_fusion.2 = f32[9]{0:T(128)S(1)} fusion(f32[64,9]{0,1:T(8,128)S(1)} %reshape.428, s32[]{:T(128)} %bitcast.1), kind=kOutput, calls=%fused_computation.18 | convolution fusion | flops 6976 | bytes 2344 | tf_op jit(solution)/shard_map/dot_general | solution.py:252
  8.2 0.1 slice.25
  8.2 0.1 slice.26
  8.3 0.1 copy.33
  8.4 0.1 broadcast_in_dim.9
  8.5 0.1 reshape.430
  8.6 1.3 %fusion.13 = f32[512,128]{1,0:T(8,128)S(1)} fusion(f32[3,128]{1,0:T(4,128)S(1)} %reshape.430, f32[128]{0:T(128)S(1)} %maximum_subtract_fusion, s32[3,512]{1,0:T(4,128)} %param.14), kind=kOutput, calls=%fused_computation.13 | convolution fusion | flops 2624512 | bytes 270336 | tf_op jit(solution)/shard_map/dot_general | solution.py:267
  9.9 0.0 copy-start.7
  9.9 0.8 %fusion.18 = (bf16[512,64]{1,0:T(8,128)(2,1)S(1)}, bf16[512,64]{1,0:T(8,128)(2,1)}) fusion(f32[512,128]{1,0:T(8,128)S(1)} %fusion.13), kind=kLoop, calls=%fused_computation.24 | loop fusion | flops 131072 | bytes 262144 | tf_op jit(solution)/shard_map/convert.1
  10.7 0.9 %fusion.16 = f32[64,512]{1,0:T(8,128)S(1)} fusion(f32[64]{0:T(128)S(1)} %iota_subtract_fusion, f32[3]{0:T(128)S(1)} %bitcast.70, s32[3,512]{1,0:T(4,128)} %param.14), kind=kOutput, calls=%fused_computation.17 | convolution fusion | flops 1313792 | bytes 137484 | tf_op jit(solution)/shard_map/dot_general | solution.py:269
  11.6 0.0 copy-done.7
  11.7 2.0 %fusion.68 = f32[144,512]{1,0:T(8,128)} fusion(f32[144,64]{1,0:T(8,128)} %constant.88.clone, f32[64,512]{1,0:T(8,128)S(1)} %fusion.16), kind=kOutput, calls=%fused_computation.104 | convolution fusion | flops 56623104 | bytes 462848 | tf_op jit(solution)/shard_map/dot_general | solution.py:279
  13.6 1.1 %reshape.429.l_ref = f32[72,1024]{1,0:T(8,128)S(1)} reshape(f32[144,512]{1,0:T(8,128)} %fusion.68) | data formatting | bytes 589824 | tf_op jit(solution)/shard_map/reshape | solution.py:279
  14.7 0.0 copy-done
  14.7 0.0 copy-done.14
  14.7 1.3 %fusion.17 = (bf16[512,64]{1,0:T(8,128)(2,1)S(1)}, bf16[512,64]{1,0:T(8,128)(2,1)S(1)}) fusion(f32[64]{0:T(128)S(1)} %fusion.57, f32[18]{0:T(128)S(1)} %bitcast.65, s32[512]{0:T(512)S(1)} %copy-done.14, f32[512,128]{1,0:T(8,128)} %copy-done.7), kind=kOutput, calls=%fused_computation.23 | convolution fusion | flops 7283712 | bytes 264520 | tf_op jit(solution)/shard_map/dot_general | solution.py:257
  16.0 1.2 %pad_maximum_fusion = (bf16[512,192]{1,0:T(8,128)(2,1)S(1)}, bf16[512,192]{1,0:T(8,128)(2,1)S(1)}) fusion(bf16[512,64]{1,0:T(8,128)(2,1)S(1)} %get-tuple-element.8, bf16[512,64]{1,0:T(8,128)(2,1)S(1)} %get-tuple-element.7, bf16[512,64]{1,0:T(8,128)(2,1)} %get-tuple-element.6, bf16[512,64]{1,0:T(8,128)(2,1)S(1)} %get-tuple-element.5), kind=kLoop, calls=%fused_computation.25 | loop fusion | flops 1179648 | bytes 655360 | tf_op jit(solution)/shard_map/concatenate | solution.py:204
  17.2 0.0 copy-done.3
  17.3 0.0 copy-done.6
  17.3 0.0 copy-done.1
  17.3 0.0 copy-done.4
  17.3 0.0 copy-done.5
  17.3 0.0 copy-done.2
  17.3 23.8 %shard_map.118 = f32[128,2048]{1,0:T(8,128)S(1)} custom-call(f32[2,64,2048]{2,1,0:T(8,128)S(1)} %bitcast.67, bf16[384,256]{1,0:T(8,128)(2,1)S(1)} %copy-done.3, bf16[64,128]{1,0:T(8,128)(2,1)S(1)} %copy-done.6, f32[72,1024]{1,0:T(8,128)S(1)} %reshape.429.l_ref, bf16[512,192]{1,0:T(8,128)(2,1)S(1)} %get-tuple-element.19.y_ref, ...), custom_call_target="tpu_custom_call" | custom-call | tf_op jit(solution)/shard_map/pallas_call | solution.py:219
  41.2 0.8 %copy.36 = f32[1,2,64,2048]{3,1,0,2:T(2,128)S(1)} copy(f32[1,2,64,2048]{3,2,1,0:T(8,128)S(1)} %bitcast.66) | data formatting | bytes 2097152 | tf_op jit(solution)/shard_map/reshape | solution.py:288
  42.0 4.6 %all_to_all.15 = f32[1,2,64,2048]{3,1,0,2:T(2,128)S(1)} all-to-all(f32[1,2,64,2048]{3,1,0,2:T(2,128)S(1)} %copy.36), channel_id=1, replica_groups=mesh['grp'=2,'rec'=4,'chan'=2,'fft'=2] {'fft'}, dimensions={2} | all-to-all | bytes 2097152 | tf_op jit(solution)/shard_map/all_to_all | solution.py:290
  46.5 0.6 %copy.37 = f32[1,2,64,2048]{3,2,1,0:T(8,128)S(1)} copy(f32[1,2,64,2048]{3,1,0,2:T(2,128)S(1)} %all_to_all.15) | data formatting | bytes 2097152 | tf_op jit(solution)/shard_map/all_to_all | solution.py:290
  47.2 0.8 %copy.38 = f32[1,2,32,2,2048]{4,3,2,1,0:T(2,128)S(1)} copy(f32[1,2,32,2,2048]{4,2,3,1,0:T(8,128)S(1)} %bitcast.68) | data formatting | bytes 2097152 | tf_op jit(solution)/shard_map/all_to_all | solution.py:290
  48.0 0.0 copy-start.12
  48.0 0.0 copy-start.13
  48.0 1.2 %reshape.432 = f32[2,32,64,64]{3,2,1,0:T(8,128)S(1)} reshape(f32[1,2,32,2,2048]{4,3,2,1,0:T(2,128)S(1)} %copy.38) | data formatting | bytes 2097152 | tf_op jit(solution)/shard_map/reshape | solution.py:291
  49.2 0.0 copy-done.12
  49.2 0.0 copy-done.13
  49.2 0.0 copy-start.10
  49.2 0.0 copy-start.11
  49.2 0.7 %fusion.7 = f32[2,32,32,64]{3,2,0,1:T(8,128)S(1)} fusion(f32[1,2,64,32]{2,3,1,0:T(8,128)S(1)} %copy-done.13, f32[1,2,64,32]{2,3,1,0:T(8,128)S(1)} %copy-done.12, f32[2,32,64,64]{3,2,1,0:T(8,128)S(1)} %reshape.432), kind=kOutput, calls=%fused_computation.5 | convolution fusion | flops 100671488 | bytes 1605632 | tf_op jit(solution)/shard_map/dcky,cxkz->dxyz/dot_general | solution.py:298
  49.9 0.0 copy-done.8
  49.9 0.0 copy-done.9
  50.0 0.6 convolution_bitcast_fusion
  50.6 0.2 reshape.434
  50.7 1.5 %collective-permute-start.1 = (f32[1,32,2048]{2,1,0:T(8,128)S(1)}, f32[1,32,2048]{2,1,0:T(8,128)S(1)}, u32[]{:S(2)}, u32[]{:S(2)}) collective-permute-start(f32[1,32,2048]{2,1,0:T(8,128)S(1)} %reshape.434), channel_id=1, source_target_pairs={{0,2},{2,0},{1,3},{3,1},{4,6},{6,4},{5,7},{7,5},{8,10},{10,8},{9,1... | collective-permute-start | bytes 786440 | tf_op jit(solution)/shard_map/ppermute | solution.py:22
  52.3 0.0 copy-done.10
  52.3 0.0 copy-done.11
  52.3 0.7 %fusion.4 = f32[2,32,32,64]{3,2,0,1:T(8,128)S(1)} fusion(f32[1,2,64,32]{2,3,1,0:T(8,128)S(1)} %copy-done.11, f32[1,2,64,32]{2,3,1,0:T(8,128)S(1)} %copy-done.10, f32[2,32,64,64]{3,2,1,0:T(8,128)S(1)} %reshape.432), kind=kOutput, calls=%fused_computation.4 | convolution fusion | flops 100671488 | bytes 1605632 | tf_op jit(solution)/shard_map/dcky,cxkz->dxyz/dot_general | solution.py:298
  53.0 0.6 convolution_bitcast_fusion.1
  53.6 0.2 reshape.433
  53.8 5.4 %collective-permute-done.1 = f32[1,32,2048]{2,1,0:T(8,128)S(1)} collective-permute-done((f32[1,32,2048]{2,1,0:T(8,128)S(1)}, f32[1,32,2048]{2,1,0:T(8,128)S(1)}, u32[]{:S(2)}, u32[]{:S(2)}) %collective-permute-start.1) | collective-permute-done | bytes 262176 | tf_op jit(solution)/shard_map/ppermute | solution.py:22
  59.2 0.7 %add.134 = f32[1,32,2048]{2,1,0:T(8,128)} add(f32[1,32,2048]{2,1,0:T(8,128)S(1)} %reshape.433, f32[1,32,2048]{2,1,0:T(8,128)S(1)} %collective-permute-done.1) | non-fusion elementwise | flops 65536 | bytes 786432 | tf_op jit(solution)/shard_map/add | solution.py:308
  (7 shorter events, 0.0 us)
Async XLA Ops:
  0.0 14.7 %copy-start = (f32[18,1]{0,1:T(1,128)S(1)}, f32[18,1]{0,1:T(1,128)}, u32[]{:S(2)}) copy-start(f32[18,1]{0,1:T(1,128)} %param.16) | copy-start | bytes 220
  0.0 17.2 %copy-start.3 = (bf16[384,256]{1,0:T(8,128)(2,1)S(1)}, bf16[384,256]{1,0:T(8,128)(2,1)}, u32[]{:S(2)}) copy-start(bf16[384,256]{1,0:T(8,128)(2,1)} %constant.89.clone.flip_ref) | copy-start | bytes 589828
  0.0 17.2 %copy-start.6 = (bf16[64,128]{1,0:T(8,128)(2,1)S(1)}, bf16[64,128]{1,0:T(8,128)(2,1)}, u32[]{:S(2)}) copy-start(bf16[64,128]{1,0:T(8,128)(2,1)} %constant.90.clone.rows_ref) | copy-start | bytes 49156
  0.0 17.3 %copy-start.1 = (bf16[8,192,512]{2,1,0:T(8,128)(2,1)S(1)}, bf16[8,192,512]{2,1,0:T(8,128)(2,1)}, u32[]{:S(2)}) copy-start(bf16[8,192,512]{2,1,0:T(8,128)(2,1)} %constant.91.clone.yt_ref) | copy-start | bytes 4718596
  0.0 17.3 %copy-start.4 = (bf16[192,512]{1,0:T(8,128)(2,1)S(1)}, bf16[192,512]{1,0:T(8,128)(2,1)}, u32[]{:S(2)}) copy-start(bf16[192,512]{1,0:T(8,128)(2,1)} %constant.92.clone.zt_ref) | copy-start | bytes 589828
  0.0 17.3 %copy-start.5 = (f32[128,72]{1,0:T(8,128)S(1)}, f32[128,72]{1,0:T(8,128)}, u32[]{:S(2)}) copy-start(f32[128,72]{1,0:T(8,128)} %constant.93.clone.turn_ref) | copy-start | bytes 110596
  0.0 14.7 %copy-start.14 = (s32[512]{0:T(512)S(1)}, s32[512]{0:T(512)}, u32[]{:S(2)}) copy-start(s32[512]{0:T(512)} %param.15) | copy-start | bytes 6148
  0.0 17.2 %copy-start.2 = (f32[1,1,2,64,2048]{4,3,2,1,0:T(8,128)S(1)}, f32[1,1,2,64,2048]{4,3,2,1,0:T(8,128)}, u32[]{:S(2)}) copy-start(f32[1,1,2,64,2048]{4,3,2,1,0:T(8,128)} %param.17) | copy-start | bytes 3145732
  0.1 7.3 %collective-permute-start = (s32[1]{0:T(128)}, s32[1]{0:T(128)}, u32[]{:S(2)}, u32[]{:S(2)}) collective-permute-start(s32[1]{0:T(128)} %param.12), channel_id=1, source_target_pairs={{0,8},{4,12},{8,0},{12,4},{1,9},{5,13},{9,1},{13,5},{2,10},{6,14},... | collective-permute-start | bytes 20 | tf_op jit(solution)/shard_map/ppermute | solution.py:22
  9.9 1.7 %copy-start.7 = (f32[512,128]{1,0:T(8,128)}, f32[512,128]{1,0:T(8,128)S(1)}, u32[]{:S(2)}) copy-start(f32[512,128]{1,0:T(8,128)S(1)} %fusion.13) | copy-start | bytes 786436
  48.0 1.2 %copy-start.12 = (f32[1,2,64,32]{2,3,1,0:T(8,128)S(1)}, f32[1,2,64,32]{2,3,1,0:T(8,128)}, u32[]{:S(2)}) copy-start(f32[1,2,64,32]{2,3,1,0:T(8,128)} %get-tuple-element.9) | copy-start | bytes 49156
  48.0 1.2 %copy-start.13 = (f32[1,2,64,32]{2,3,1,0:T(8,128)S(1)}, f32[1,2,64,32]{2,3,1,0:T(8,128)}, u32[]{:S(2)}) copy-start(f32[1,2,64,32]{2,3,1,0:T(8,128)} %get-tuple-element.10) | copy-start | bytes 49156
  49.2 0.8 %copy-start.8 = (f32[1,64,64]{2,1,0:T(8,128)S(1)}, f32[1,64,64]{2,1,0:T(8,128)}, u32[]{:S(2)}) copy-start(f32[1,64,64]{2,1,0:T(8,128)} %get-tuple-element.23) | copy-start | bytes 49156
  49.2 0.8 %copy-start.9 = (f32[1,64,64]{2,1,0:T(8,128)S(1)}, f32[1,64,64]{2,1,0:T(8,128)}, u32[]{:S(2)}) copy-start(f32[1,64,64]{2,1,0:T(8,128)} %get-tuple-element.24) | copy-start | bytes 49156
  49.2 3.1 %copy-start.10 = (f32[1,2,64,32]{2,3,1,0:T(8,128)S(1)}, f32[1,2,64,32]{2,3,1,0:T(8,128)}, u32[]{:S(2)}) copy-start(f32[1,2,64,32]{2,3,1,0:T(8,128)} %get-tuple-element.11) | copy-start | bytes 49156
  49.2 3.1 %copy-start.11 = (f32[1,2,64,32]{2,3,1,0:T(8,128)S(1)}, f32[1,2,64,32]{2,3,1,0:T(8,128)}, u32[]{:S(2)}) copy-start(f32[1,2,64,32]{2,3,1,0:T(8,128)} %get-tuple-element.12) | copy-start | bytes 49156
  50.7 8.5 %collective-permute-start.1 = (f32[1,32,2048]{2,1,0:T(8,128)S(1)}, f32[1,32,2048]{2,1,0:T(8,128)S(1)}, u32[]{:S(2)}, u32[]{:S(2)}) collective-permute-start(f32[1,32,2048]{2,1,0:T(8,128)S(1)} %reshape.434), channel_id=1, source_target_pairs={{0,2},{2,0},{1,3},{3,1},{4,6},{6,4},{5,7},{7,5},{8,10},{10,8},{9,1... | collective-permute-start | bytes 786440 | tf_op jit(solution)/shard_map/ppermute | solution.py:22

commit v5 on v4

--- a/solution.py
+++ b/solution.py
@@ -22,12 +22,6 @@
     return lax.ppermute(value, axis, pairs)
 
 
-def waves(rows, columns):
-    phase = rows[:, None] * columns[None, :] % GRID
-    angle = phase.astype(jnp.float32) * (2.0 * math.pi / GRID)
-    return jnp.cos(angle), jnp.sin(angle)
-
-
 def host_waves(rows, columns):
     angle = (np.outer(rows, columns) % GRID) * (2.0 * np.pi / GRID)
     return np.cos(angle), np.sin(angle)
@@ -37,7 +31,7 @@
     table = table.astype(np.float32)
     high = table.astype(jnp.bfloat16)
     low = (table - high.astype(np.float32)).astype(jnp.bfloat16)
-    return np.concatenate([high, high, low], axis=0)
+    return np.concatenate([high, high, low, np.zeros_like(low)], axis=0)
 
 
 ROWS = 72
@@ -54,8 +48,8 @@
 
 
 def window_kernel(
-    count, s_ref, flip_ref, rows_ref, l_ref, y_ref, z_ref, yt_ref, zt_ref, turn_ref, out_ref,
-    source, own, first, pair, second, win, lig, z_wave, l_high, l_low,
+    count, s_ref, flip_ref, rows_ref, xt_ref, x_ref, hat_ref, weight_ref, yt_ref, zt_ref, turn_ref, out_ref,
+    source, own, first, pair, second, win, lig, y_cols, z_wave, l_high, l_low,
     send0, recv0, send1, recv1, send2, recv2, send3, recv3,
 ):
     grp = lax.axis_index("grp")
@@ -106,10 +100,23 @@
     for copy in zeros:
         copy.start()
 
-    z_wave[...] = dot(z_ref[...], zt_ref[...])
-    high, low = split(l_ref[...])
-    l_high[...] = high
-    l_low[...] = low
+    def columns(value):
+        high = value.astype(jnp.bfloat16)
+        rounded = high.astype(jnp.float32)
+        lane = lax.broadcasted_iota(jnp.int32, value.shape, 1)
+        mixed = jnp.where(lane < GRID, rounded, value - rounded).astype(jnp.bfloat16)
+        return jnp.concatenate([mixed, high], axis=1)
+
+    y_cols[...] = columns(hat_ref[:, 0:128] * weight_ref[...])
+    z_wave[...] = dot(columns(hat_ref[:, 128:256]), zt_ref[...])
+    x_high, x_low = split(x_ref[...])
+    atoms = x_ref.shape[1]
+    for part in range(2):
+        xt_high, xt_low = split(xt_ref[part])
+        left = dot(xt_high, x_high) + dot(xt_low, x_high) + dot(xt_high, x_low)
+        high, low = split(left)
+        l_high[:, part * atoms : (part + 1) * atoms] = high
+        l_low[:, part * atoms : (part + 1) * atoms] = low
 
     def fold(c):
         chunk = base + c
@@ -125,7 +132,7 @@
         own[c, 64:72] = jnp.where(row == 0, re, jnp.where(row == 1, im, 0.0))
 
     def ligand(chunk):
-        y_wave = dot(y_ref[...], yt_ref[chunk])
+        y_wave = dot(y_cols[...], yt_ref[chunk])
         y_re, y_im = y_wave[:, :LANES], y_wave[:, LANES:]
         z_re, z_im = z_wave[:, :LANES], z_wave[:, LANES:]
         re_high, re_low = split(y_re * z_re - y_im * z_im)
@@ -177,7 +184,7 @@
         copy.wait_send()
 
 
-def turned_product(receptor, left, y_hat, z_hat, width):
+def turned_product(receptor, table, x_hat, hats, weights, width):
     index = np.arange(GRID)
     chunks = width // LANES
     lane = np.arange(width)
@@ -199,10 +206,6 @@
     turn = np.concatenate([real, imag], axis=0) / float(GRID**3)
     turn = np.pad(turn, ((0, 0), (0, ROWS - turn.shape[1]))).astype(np.float32)
 
-    def columns(value):
-        high = lax.reduce_precision(value, 8, 7)
-        return jnp.concatenate([high, value - high, high], axis=1).astype(jnp.bfloat16)
-
     flip = np.zeros((384, LANES), np.float32)
     for m in range(LANES // GRID):
         for kz in range(GRID):
@@ -213,13 +216,13 @@
         rows[kx, HALF - kx] = 1.0
         rows[HALF + kx, 2 * HALF - kx] = -1.0
     rows = np.concatenate([rows, rows], axis=1).astype(jnp.bfloat16)
-    atoms = y_hat.shape[0]
+    atoms = hats.shape[0]
     piece = (ROWS, LANES)
     half = chunks // 2
     return pl.pallas_call(
         functools.partial(window_kernel, lax.axis_size("rec")),
         out_shape=jax.ShapeDtypeStruct((2 * GRID, width), jnp.float32),
-        in_specs=[pl.BlockSpec(memory_space=pltpu.VMEM)] * 9,
+        in_specs=[pl.BlockSpec(memory_space=pltpu.VMEM)] * 10,
         out_specs=pl.BlockSpec(memory_space=pltpu.VMEM),
         scratch_shapes=[
             pltpu.VMEM((2 * HALF, width + 128), jnp.float32),
@@ -229,6 +232,7 @@
             pltpu.VMEM((half,) + piece, jnp.float32),
             pltpu.VMEM((chunks,) + piece, jnp.float32),
             pltpu.VMEM((chunks,) + piece, jnp.float32),
+            pltpu.VMEM((atoms, 4 * GRID), jnp.bfloat16),
             pltpu.VMEM((atoms, 2 * LANES), jnp.float32),
             pltpu.VMEM((ROWS, 2 * atoms), jnp.bfloat16),
             pltpu.VMEM((ROWS, 2 * atoms), jnp.bfloat16),
@@ -239,7 +243,7 @@
             collective_id=0, has_side_effects=True, vmem_limit_bytes=40 * 1024 * 1024
         ),
     )(
-        receptor, jnp.asarray(flip), jnp.asarray(rows), left, columns(y_hat), columns(z_hat),
+        receptor, jnp.asarray(flip), jnp.asarray(rows), table, x_hat, hats, weights,
         jnp.asarray(y_table), jnp.asarray(z_table), jnp.asarray(turn),
     )
 
@@ -254,56 +258,55 @@
     type_hot = (atom_types[:, None] == jnp.arange(kinds, dtype=jnp.int32)[None, :]).astype(
         jnp.float32
     )
+    odd = (jnp.arange(2 * GRID, dtype=jnp.int32) * lax.axis_index("fft")) % 2
+    sign = 1.0 - 2.0 * odd.astype(jnp.float32)[None, :]
     weights = jnp.dot(
-        type_hot, jnp.broadcast_to(channel_weights, (kinds, GRID)), precision=HIGHEST
+        type_hot, jnp.broadcast_to(channel_weights, (kinds, 2 * GRID)) * sign, precision=HIGHEST
     )
     coords = ligand_coords.astype(jnp.float32) * (1.0 / 256.0)
     matrix = matrix.reshape(3, 3)
     center = 0.5 * GRID
     cells = jnp.arange(GRID, dtype=jnp.float32)
-    offset = center - jnp.concatenate([cells, cells])
-    spread = jnp.repeat(matrix[1:].T, GRID, axis=1)
+    offset = center - jnp.concatenate([cells] * 4)
+    spread = jnp.repeat(matrix[1:].T, 2 * GRID, axis=1)
     hats = jnp.maximum(
         0.0, 1.0 - jnp.abs(jnp.dot(coords.T, spread, precision=HIGHEST) + offset[None, :])
     )
     x_places = jnp.dot(jnp.broadcast_to(matrix[0], (GRID, 3)), coords, precision=HIGHEST)
     x_hat = jnp.maximum(0.0, 1.0 - jnp.abs(x_places + (center - cells)[:, None]))
-    odd = (jnp.arange(GRID, dtype=jnp.int32) * lax.axis_index("fft")) % 2
-    y_hat = hats[:, :GRID] * weights * (1.0 - 2.0 * odd.astype(jnp.float32))
-    z_hat = hats[:, GRID:]
     cosine, sine = host_waves(np.arange(HALF + 1), np.arange(GRID))
     none = np.zeros((6, GRID))
     meet_re = np.concatenate([cosine[:HALF], sine[:HALF], cosine[HALF:], sine[HALF:], none], 0)
     meet_im = np.concatenate([-sine[:HALF], cosine[:HALF], -sine[HALF:], cosine[HALF:], none], 0)
-    table = jnp.asarray(np.stack([meet_re, meet_im], axis=1).reshape(2 * ROWS, GRID), jnp.float32)
-    left = jnp.dot(table, x_hat, precision=HIGHEST).reshape(ROWS, 2 * x_hat.shape[1])
-    return left, y_hat, z_hat
+    table = jnp.asarray(np.stack([meet_re, meet_im]), jnp.float32)
+    return table, x_hat, hats, weights
 
 
 def body(record_ids, rotations, ligand_coords, atom_types, channel_weights, receptor_spectra):
     width = receptor_spectra.shape[-1]
     slab = GRID // lax.axis_size("fft")
     record = from_behind(record_ids, "rec", 2)
-    left, y_hat, z_hat = hats_of(record, rotations, ligand_coords, atom_types, channel_weights)
-    turned = turned_product(receptor_spectra[0, 0], left, y_hat, z_hat, width).reshape(1, 2, GRID, width)
-    index = jnp.arange(GRID, dtype=jnp.int32)
+    parts = hats_of(record, rotations, ligand_coords, atom_types, channel_weights)
+    turned = turned_product(receptor_spectra[0, 0], *parts, width).reshape(1, 2, GRID, width)
+    index = np.arange(GRID)
     halves = lax.all_to_all(turned, "fft", split_axis=2, concat_axis=3, tiled=True)
     volume = halves.reshape(2, slab, GRID, GRID)
-    cosine, sine = waves(index, index)
-    z_turn = jnp.stack([cosine, -sine])
-
-    def scores(places):
-        y_cos, y_sin = waves(index, places)
-        y_turn = jnp.stack([jnp.stack([y_cos, -y_sin]), jnp.stack([y_sin, y_cos])])
+    cosine, sine = host_waves(index, index)
+    z_turn = jnp.asarray(np.stack([cosine, -sine]), jnp.float32)
+    y_all = np.stack([np.stack([cosine, -sine]), np.stack([sine, cosine])])
+
+    def scores(y_turn):
         in_y = jnp.einsum("dcky,cxkz->dxyz", y_turn, volume, precision=HIGH)
         part = jnp.einsum("dxyz,dzt->xyt", in_y, z_turn, precision=HIGH)
-        return part.reshape(1, slab, places.shape[0] * GRID)
+        return part.reshape(1, slab, y_turn.shape[3] * GRID)
 
     count = lax.axis_size("chan")
     if count != 2:
-        return lax.psum_scatter(scores(index), "chan", scatter_dimension=2, tiled=True)
-    near = lax.axis_index("chan") * HALF + jnp.arange(HALF, dtype=jnp.int32)
-    far = (near + HALF) % GRID
+        return lax.psum_scatter(scores(jnp.asarray(y_all, jnp.float32)), "chan", scatter_dimension=2, tiled=True)
+    halves_y = jnp.asarray(np.stack([y_all[..., :HALF], y_all[..., HALF:]]), jnp.float32)
+    me = lax.axis_index("chan")
+    near = lax.dynamic_index_in_dim(halves_y, me, 0, keepdims=False)
+    far = lax.dynamic_index_in_dim(halves_y, 1 - me, 0, keepdims=False)
     arrived = from_behind(scores(far), "chan", 1)
     return scores(near) + arrived
 

time: 60.4 us -> 60.2 us (level)
  local copies, waits for them, and re-layouts: 6.06 us -> 12.1 us
  other arithmetic: 5.2 us -> 0.83 us
  matrix products: 8.89 us -> 6.61 us
    unnamed x30 -> x19, local copies, waits for them, and re-layouts: 0.1 us -> 7.35 us
    dot_general x2 -> x1, matrix products: 3.27 us -> 1.01 us  [hats_of(): jnp.dot(type_hot, jnp.broadcast_to(channel_weights, (kinds, 2 * GRID)) *...]
    another operation x3 -> x0, other arithmetic: 2.05 us -> none  [the longest x2 1.27 us: scores(): y_turn = jnp.stack([jnp.stack([y_cos, -y_sin]), jnp.stack([y_sin, y_cos])])]
    concatenate x1 -> x0, other arithmetic: 1.23 us -> none  [columns(): jnp.concatenate([high, value - high, high], axis=1).astype(jnp.bfloat16)]
    reshape x5 -> x3, local copies, waits for them, and re-layouts: 2.32 us -> 1.18 us  [the longest x1 0.81 us: body(): turned_product(receptor_spectra[0, 0], *parts, width)]
    neg x3 -> x0, other arithmetic: 1.08 us -> none  [the longest x1 0.77 us: body(): z_turn = jnp.stack([cosine, -sine])]
  transfers between devices with their start and end apart: 2 -> 2, of which waited for: 1 -> 1; matrix products, arithmetic and copies ran while one was open for 8% -> 5% of each run, Pallas kernels for 0% -> 0%
where the time goes in v5:
time: 60.2 us; the launch traced here: 59.6 us
  Pallas kernels  24.3 us (40%)
  local copies, waits for them, and re-layouts  12.1 us (20%)
  matrix products  6.61 us (11%)
  starting transfers between devices  5.58 us (9%)
  waiting for transfers between devices  5.44 us (9%)
  blocking collectives  4.58 us (8%)
  other arithmetic  0.83 us (1%)
    pallas_call x1, Pallas kernels, turned_product(): pl.pallas_call(functools.partial(window_kernel, lax.axis_size('rec')), ou...  24.3 us
    unnamed x19, local copies, waits for them, and re-layouts  7.35 us
    ppermute x2, starting transfers between devices, from_behind(): return lax.ppermute(value, axis, pairs)  5.58 us
    ppermute x2, waiting for transfers between devices, from_behind(): return lax.ppermute(value, axis, pairs)  5.44 us
    all_to_all x1, blocking collectives, body(): lax.all_to_all(turned, 'fft', split_axis=2, concat_axis=3, tiled=True)  4.58 us
    all_to_all x2, local copies, waits for them, and re-layouts, body(): lax.all_to_all(turned, 'fft', split_axis=2, concat_axis=3, tiled=True)  1.42 us
    dot_general x2, matrix products, scores(): in_y = jnp.einsum('dcky,cxkz->dxyz', y_turn, volume, precision=HIGH)  1.37 us
    dot_general x1, matrix products, hats_of(): jnp.dot(coords.T, spread, precision=HIGHEST) + offset[None, :]  1.35 us
  transfers between devices with their start and end apart: 2, of which 1 were waited for; matrix products, arithmetic and copies ran while one was open for 5% of the time, Pallas kernels for 0%

profile of v5, /device:TPU:0, one launch (start us, length us, event | category | flops | bytes accessed | tf_op | source)
XLA Modules:
  0.0 59.6 jit_solution(14476766618528253252)
XLA Ops:
  0.0 4.0 %collective-permute-start = (s32[1]{0:T(128)}, s32[1]{0:T(128)}, u32[]{:S(2)}, u32[]{:S(2)}) collective-permute-start(s32[1]{0:T(128)} %param.14), channel_id=1, source_target_pairs={{0,8},{4,12},{8,0},{12,4},{1,9},{5,13},{9,1},{13,5},{2,10},{6,14},... | collective-permute-start | bytes 20 | tf_op jit(solution)/shard_map/ppermute | solution.py:22
  4.0 0.7 %reshape.94 = f32[64,9]{0,1:T(8,128)S(1)} reshape(f32[64,3,3]{0,2,1:T(4,128)} %param.15) | data formatting | bytes 4608 | tf_op jit(solution)/shard_map/reshape | solution.py:256
  4.8 0.1 maximum_subtract_fusion
  4.8 1.0 %fusion.16.weight_ref = f32[512,128]{1,0:T(8,128)S(1)} fusion(s32[512]{0:T(512)} %param.17, f32[128]{0:T(128)S(1)} %fusion.34, f32[18]{0:T(128)} %bitcast.64), kind=kOutput, calls=%fused_computation.18 | convolution fusion | flops 14167296 | bytes 264776 | tf_op jit(solution)/shard_map/dot_general | solution.py:263
  5.9 0.0 collective-permute-done
  5.9 0.7 %convolution_bitcast_fusion.2 = f32[9]{0:T(128)S(1)} fusion(f32[64,9]{0,1:T(8,128)S(1)} %reshape.94, s32[]{:T(128)} %bitcast.1), kind=kOutput, calls=%fused_computation.16 | convolution fusion | flops 6976 | bytes 2344 | tf_op jit(solution)/shard_map/dot_general | solution.py:256
  6.6 0.1 slice.19
  6.7 0.1 slice.20
  6.8 0.1 copy.21
  6.9 0.1 broadcast_bitcast_fusion
  7.0 1.4 %fusion.12.hat_ref = f32[512,256]{1,0:T(8,128)S(1)} fusion(f32[256]{0:T(256)S(1)} %maximum_subtract_fusion, s32[3,512]{1,0:T(4,128)} %param.16, f32[1,3,2,128]{3,2,1,0:T(2,128)S(1)} %broadcast_bitcast_fusion), kind=kOutput, calls=%fused_computation.9 | convolution fusion | flops 5245952 | bytes 534528 | tf_op jit(solution)/shard_map/dot_general | solution.py:273
  8.3 0.9 %fusion.15.x_ref = f32[64,512]{1,0:T(8,128)S(1)} fusion(f32[64]{0:T(128)S(1)} %iota_subtract_fusion, f32[3]{0:T(128)S(1)} %bitcast.65, s32[3,512]{1,0:T(4,128)} %param.16), kind=kOutput, calls=%fused_computation.15 | convolution fusion | flops 1313792 | bytes 137484 | tf_op jit(solution)/shard_map/dot_general | solution.py:275
  9.3 0.0 copy-start
  9.3 1.6 %copy-done = bf16[8,256,512]{2,1,0:T(8,128)(2,1)S(1)} copy-done((bf16[8,256,512]{2,1,0:T(8,128)(2,1)S(1)}, bf16[8,256,512]{2,1,0:T(8,128)(2,1)}, u32[]{:S(2)}) %copy-start) | copy-done | bytes 2097176
  10.9 0.0 copy-start.1
  10.9 1.2 %copy-done.1 = f32[1,1,2,64,2048]{4,3,2,1,0:T(8,128)S(1)} copy-done((f32[1,1,2,64,2048]{4,3,2,1,0:T(8,128)S(1)}, f32[1,1,2,64,2048]{4,3,2,1,0:T(8,128)}, u32[]{:S(2)}) %copy-start.1) | copy-done | bytes 1048600
  12.1 0.0 copy-start.2
  12.1 0.9 %copy-done.2 = bf16[256,512]{1,0:T(8,128)(2,1)S(1)} copy-done((bf16[256,512]{1,0:T(8,128)(2,1)S(1)}, bf16[256,512]{1,0:T(8,128)(2,1)}, u32[]{:S(2)}) %copy-start.2) | copy-done | bytes 262168
  13.0 0.0 copy-start.3
  13.0 0.9 %copy-done.3 = bf16[384,256]{1,0:T(8,128)(2,1)S(1)} copy-done((bf16[384,256]{1,0:T(8,128)(2,1)S(1)}, bf16[384,256]{1,0:T(8,128)(2,1)}, u32[]{:S(2)}) %copy-start.3) | copy-done | bytes 196632
  14.0 0.0 copy-start.4
  14.0 0.9 %copy-done.4 = f32[2,72,64]{2,1,0:T(8,128)S(1)} copy-done((f32[2,72,64]{2,1,0:T(8,128)S(1)}, f32[2,72,64]{2,1,0:T(8,128)}, u32[]{:S(2)}) %copy-start.4) | copy-done | bytes 36888
  14.9 0.0 copy-start.5
  14.9 0.8 %copy-done.5 = f32[128,72]{1,0:T(8,128)S(1)} copy-done((f32[128,72]{1,0:T(8,128)S(1)}, f32[128,72]{1,0:T(8,128)}, u32[]{:S(2)}) %copy-start.5) | copy-done | bytes 36888
  15.7 0.0 copy-start.6
  15.7 0.7 %copy-done.6 = bf16[64,128]{1,0:T(8,128)(2,1)S(1)} copy-done((bf16[64,128]{1,0:T(8,128)(2,1)S(1)}, bf16[64,128]{1,0:T(8,128)(2,1)}, u32[]{:S(2)}) %copy-start.6) | copy-done | bytes 16408
  16.4 24.3 %shard_map.136 = f32[128,2048]{1,0:T(8,128)S(1)} custom-call(f32[2,64,2048]{2,1,0:T(8,128)S(1)} %bitcast.61, bf16[384,256]{1,0:T(8,128)(2,1)S(1)} %copy-done.3, bf16[64,128]{1,0:T(8,128)(2,1)S(1)} %copy-done.6, f32[2,72,64]{2,1,0:T(8,128)S(1)} %copy-done.4, f32[64,512]{1,0:T(8,128)S(1)} %fusion.15.x_ref, f32[512,256]{1,0:T(8,128)S(1)} %fusion.12.hat_ref, ...), custom_call_target="tpu_custom_call" | custom-call | tf_op jit(solution)/shard_map/pallas_call | solution.py:222
  40.8 0.8 %copy.22 = f32[1,2,64,2048]{3,1,0,2:T(2,128)S(1)} copy(f32[1,2,64,2048]{3,2,1,0:T(8,128)S(1)} %bitcast.60) | data formatting | bytes 2097152 | tf_op jit(solution)/shard_map/reshape | solution.py:290
  41.6 4.6 %all_to_all.15 = f32[1,2,64,2048]{3,1,0,2:T(2,128)S(1)} all-to-all(f32[1,2,64,2048]{3,1,0,2:T(2,128)S(1)} %copy.22), channel_id=1, replica_groups=mesh['grp'=2,'rec'=4,'chan'=2,'fft'=2] {'fft'}, dimensions={2} | all-to-all | bytes 2097152 | tf_op jit(solution)/shard_map/all_to_all | solution.py:292
  46.2 0.6 %copy.23 = f32[1,2,64,2048]{3,2,1,0:T(8,128)S(1)} copy(f32[1,2,64,2048]{3,1,0,2:T(2,128)S(1)} %all_to_all.15) | data formatting | bytes 2097152 | tf_op jit(solution)/shard_map/all_to_all | solution.py:292
  46.8 0.0 copy-start.8
  46.8 0.8 %copy.24 = f32[1,2,32,2,2048]{4,3,2,1,0:T(2,128)S(1)} copy(f32[1,2,32,2,2048]{4,2,3,1,0:T(8,128)S(1)} %bitcast.62) | data formatting | bytes 2097152 | tf_op jit(solution)/shard_map/all_to_all | solution.py:292
  47.6 1.2 %reshape.97 = f32[2,32,64,64]{3,2,1,0:T(8,128)S(1)} reshape(f32[1,2,32,2,2048]{4,3,2,1,0:T(2,128)S(1)} %copy.24) | data formatting | bytes 2097152 | tf_op jit(solution)/shard_map/reshape | solution.py:293
  48.8 0.0 copy-done.8
  48.8 0.0 copy-start.7
  48.8 0.7 %fusion.7 = f32[2,32,32,64]{3,2,0,1:T(8,128)S(1)} fusion(f32[2,2,2,64,32]{3,4,2,1,0:T(8,128)S(1)} %copy-done.8, s32[]{:T(128)S(6)} %select_n.20, f32[2,32,64,64]{3,2,1,0:T(8,128)S(1)} %reshape.97), kind=kOutput, calls=%fused_computation.5 | convolution fusion | flops 100663296 | bytes 2686980 | tf_op jit(solution)/shard_map/dcky,cxkz->dxyz/dot_general | solution.py:299
  49.5 0.1 copy-done.7
  49.6 0.6 convolution_bitcast_fusion
  50.2 0.2 reshape.99
  50.4 1.5 %collective-permute-start.1 = (f32[1,32,2048]{2,1,0:T(8,128)S(1)}, f32[1,32,2048]{2,1,0:T(8,128)S(1)}, u32[]{:S(2)}, u32[]{:S(2)}) collective-permute-start(f32[1,32,2048]{2,1,0:T(8,128)S(1)} %reshape.99), channel_id=1, source_target_pairs={{0,2},{2,0},{1,3},{3,1},{4,6},{6,4},{5,7},{7,5},{8,10},{10,8},{9,1... | collective-permute-start | bytes 786440 | tf_op jit(solution)/shard_map/ppermute | solution.py:22
  52.0 0.7 %fusion.4 = f32[2,32,32,64]{3,2,0,1:T(8,128)S(1)} fusion(f32[2,2,2,64,32]{3,4,2,1,0:T(8,128)S(1)} %copy-done.8, s32[]{:T(128)S(6)} %select_n.19, f32[2,32,64,64]{3,2,1,0:T(8,128)S(1)} %reshape.97), kind=kOutput, calls=%fused_computation.4 | convolution fusion | flops 100663296 | bytes 2686980 | tf_op jit(solution)/shard_map/dcky,cxkz->dxyz/dot_general | solution.py:299
  52.6 0.6 convolution_bitcast_fusion.1
  53.2 0.2 reshape.98
  53.4 5.4 %collective-permute-done.1 = f32[1,32,2048]{2,1,0:T(8,128)S(1)} collective-permute-done((f32[1,32,2048]{2,1,0:T(8,128)S(1)}, f32[1,32,2048]{2,1,0:T(8,128)S(1)}, u32[]{:S(2)}, u32[]{:S(2)}) %collective-permute-start.1) | collective-permute-done | bytes 262176 | tf_op jit(solution)/shard_map/ppermute | solution.py:22
  58.9 0.7 %add.44 = f32[1,32,2048]{2,1,0:T(8,128)} add(f32[1,32,2048]{2,1,0:T(8,128)S(1)} %reshape.98, f32[1,32,2048]{2,1,0:T(8,128)S(1)} %collective-permute-done.1) | non-fusion elementwise | flops 65536 | bytes 786432 | tf_op jit(solution)/shard_map/add | solution.py:311
  (3 shorter events, 0.0 us)
Async XLA Ops:
  0.0 5.9 %collective-permute-start = (s32[1]{0:T(128)}, s32[1]{0:T(128)}, u32[]{:S(2)}, u32[]{:S(2)}) collective-permute-start(s32[1]{0:T(128)} %param.14), channel_id=1, source_target_pairs={{0,8},{4,12},{8,0},{12,4},{1,9},{5,13},{9,1},{13,5},{2,10},{6,14},... | collective-permute-start | bytes 20 | tf_op jit(solution)/shard_map/ppermute | solution.py:22
  9.3 1.6 %copy-start = (bf16[8,256,512]{2,1,0:T(8,128)(2,1)S(1)}, bf16[8,256,512]{2,1,0:T(8,128)(2,1)}, u32[]{:S(2)}) copy-start(bf16[8,256,512]{2,1,0:T(8,128)(2,1)} %constant.63.clone.yt_ref) | copy-start | bytes 6291460
  10.9 1.2 %copy-start.1 = (f32[1,1,2,64,2048]{4,3,2,1,0:T(8,128)S(1)}, f32[1,1,2,64,2048]{4,3,2,1,0:T(8,128)}, u32[]{:S(2)}) copy-start(f32[1,1,2,64,2048]{4,3,2,1,0:T(8,128)} %param.19) | copy-start | bytes 3145732
  12.1 0.9 %copy-start.2 = (bf16[256,512]{1,0:T(8,128)(2,1)S(1)}, bf16[256,512]{1,0:T(8,128)(2,1)}, u32[]{:S(2)}) copy-start(bf16[256,512]{1,0:T(8,128)(2,1)} %constant.64.clone.zt_ref) | copy-start | bytes 786436
  13.0 0.9 %copy-start.3 = (bf16[384,256]{1,0:T(8,128)(2,1)S(1)}, bf16[384,256]{1,0:T(8,128)(2,1)}, u32[]{:S(2)}) copy-start(bf16[384,256]{1,0:T(8,128)(2,1)} %constant.61.clone.flip_ref) | copy-start | bytes 589828
  14.0 0.9 %copy-start.4 = (f32[2,72,64]{2,1,0:T(8,128)S(1)}, f32[2,72,64]{2,1,0:T(8,128)}, u32[]{:S(2)}) copy-start(f32[2,72,64]{2,1,0:T(8,128)} %constant.60.clone.xt_ref) | copy-start | bytes 110596
  14.9 0.8 %copy-start.5 = (f32[128,72]{1,0:T(8,128)S(1)}, f32[128,72]{1,0:T(8,128)}, u32[]{:S(2)}) copy-start(f32[128,72]{1,0:T(8,128)} %constant.65.clone.turn_ref) | copy-start | bytes 110596
  15.7 0.7 %copy-start.6 = (bf16[64,128]{1,0:T(8,128)(2,1)S(1)}, bf16[64,128]{1,0:T(8,128)(2,1)}, u32[]{:S(2)}) copy-start(bf16[64,128]{1,0:T(8,128)(2,1)} %constant.62.clone.rows_ref) | copy-start | bytes 49156
  46.8 2.0 %copy-start.8 = (f32[2,2,2,64,32]{3,4,2,1,0:T(8,128)S(1)}, f32[2,2,2,64,32]{3,4,2,1,0:T(8,128)}, u32[]{:S(2)}) copy-start(f32[2,2,2,64,32]{3,4,2,1,0:T(8,128)} %constant.67.clone) | copy-start | bytes 196612
  48.8 0.8 %copy-start.7 = (f32[2,64,64,1]{2,1,0,3:T(8,128)S(1)}, f32[2,64,64,1]{2,1,0,3:T(8,128)}, u32[]{:S(2)}) copy-start(f32[2,64,64,1]{2,1,0,3:T(8,128)} %constant.71) | copy-start | bytes 98308
  50.4 8.5 %collective-permute-start.1 = (f32[1,32,2048]{2,1,0:T(8,128)S(1)}, f32[1,32,2048]{2,1,0:T(8,128)S(1)}, u32[]{:S(2)}, u32[]{:S(2)}) collective-permute-start(f32[1,32,2048]{2,1,0:T(8,128)S(1)} %reshape.99), channel_id=1, source_target_pairs={{0,2},{2,0},{1,3},{3,1},{4,6},{6,4},{5,7},{7,5},{8,10},{10,8},{9,1... | collective-permute-start | bytes 786440 | tf_op jit(solution)/shard_map/ppermute | solution.py:22

commit v6 on v5

--- a/solution.py
+++ b/solution.py
@@ -48,7 +48,7 @@
 
 
 def window_kernel(
-    count, s_ref, flip_ref, rows_ref, xt_ref, x_ref, hat_ref, weight_ref, yt_ref, zt_ref, turn_ref, out_ref,
+    count, s_ref, yt_ref, ft_ref, x_ref, hat_ref, weight_ref, out_ref,
     source, own, first, pair, second, win, lig, y_cols, z_wave, l_high, l_low,
     send0, recv0, send1, recv1, send2, recv2, send3, recv3,
 ):
@@ -108,11 +108,11 @@
         return jnp.concatenate([mixed, high], axis=1)
 
     y_cols[...] = columns(hat_ref[:, 0:128] * weight_ref[...])
-    z_wave[...] = dot(columns(hat_ref[:, 128:256]), zt_ref[...])
+    z_wave[...] = dot(columns(hat_ref[:, 128:256]), yt_ref[chunks])
     x_high, x_low = split(x_ref[...])
     atoms = x_ref.shape[1]
     for part in range(2):
-        xt_high, xt_low = split(xt_ref[part])
+        xt_high, xt_low = split(ft_ref[part * ROWS : (part + 1) * ROWS, 0:GRID])
         left = dot(xt_high, x_high) + dot(xt_low, x_high) + dot(xt_high, x_low)
         high, low = split(left)
         l_high[:, part * atoms : (part + 1) * atoms] = high
@@ -122,8 +122,10 @@
         chunk = base + c
         window = pl.ds(pl.multiple_of((2 * (chunks - 1) - 2 * chunk) * 128, 128), 384)
         high, low = split(source[:, window])
-        flipped = dot(jnp.concatenate([high, low], axis=0), flip_ref[...])
-        mirrored = dot(rows_ref[...], flipped.astype(jnp.bfloat16))
+        both = jnp.concatenate([high, low], axis=0)
+        flipped = dot(both[:, 0:256], yt_ref[chunks + 1, :, 0:LANES])
+        flipped += dot(both[:, 256:384], yt_ref[chunks + 1, 0:128, LANES : 2 * LANES])
+        mirrored = dot(yt_ref[chunks + 1, 128:192, LANES : LANES + 128], flipped.astype(jnp.bfloat16))
         lanes = pl.ds(pl.multiple_of(chunk * LANES, LANES), LANES)
         own[c, 0:32] = s_ref[0, 0:32, lanes] + mirrored[0:32]
         own[c, 32:64] = s_ref[1, 0:32, lanes] + mirrored[32:64]
@@ -143,7 +145,7 @@
             dot(l_high[...], v_high) + dot(l_low[...], v_high) + dot(l_high[...], v_low)
         )
 
-    t_high, t_low = split(turn_ref[...])
+    t_high, t_low = split(ft_ref[2 * ROWS : 2 * ROWS + 2 * GRID, 0:ROWS])
 
     def product(chunk):
         l_re, l_im = lig[chunk, 0:32], lig[chunk, 32:64]
@@ -216,13 +218,21 @@
         rows[kx, HALF - kx] = 1.0
         rows[HALF + kx, 2 * HALF - kx] = -1.0
     rows = np.concatenate([rows, rows], axis=1).astype(jnp.bfloat16)
+    moves = np.zeros((1,) + y_table.shape[1:], jnp.bfloat16)
+    moves[0, :, :LANES] = flip[:256]
+    moves[0, :128, LANES:] = flip[256:]
+    moves[0, 128:192, LANES : LANES + 128] = rows
+    constants = np.concatenate([y_table, z_table[None], moves], axis=0)
+    floats = np.zeros((2 * ROWS + 2 * GRID, 128), np.float32)
+    floats[: 2 * ROWS, :GRID] = table.reshape(2 * ROWS, GRID)
+    floats[2 * ROWS :, :ROWS] = turn
     atoms = hats.shape[0]
     piece = (ROWS, LANES)
     half = chunks // 2
     return pl.pallas_call(
         functools.partial(window_kernel, lax.axis_size("rec")),
         out_shape=jax.ShapeDtypeStruct((2 * GRID, width), jnp.float32),
-        in_specs=[pl.BlockSpec(memory_space=pltpu.VMEM)] * 10,
+        in_specs=[pl.BlockSpec(memory_space=pltpu.VMEM)] * 6,
         out_specs=pl.BlockSpec(memory_space=pltpu.VMEM),
         scratch_shapes=[
             pltpu.VMEM((2 * HALF, width + 128), jnp.float32),
@@ -243,8 +253,7 @@
             collective_id=0, has_side_effects=True, vmem_limit_bytes=40 * 1024 * 1024
         ),
     )(
-        receptor, jnp.asarray(flip), jnp.asarray(rows), table, x_hat, hats, weights,
-        jnp.asarray(y_table), jnp.asarray(z_table), jnp.asarray(turn),
+        receptor, jnp.asarray(constants), jnp.asarray(floats), x_hat, hats, weights,
     )
 
 
@@ -278,7 +287,7 @@
     none = np.zeros((6, GRID))
     meet_re = np.concatenate([cosine[:HALF], sine[:HALF], cosine[HALF:], sine[HALF:], none], 0)
     meet_im = np.concatenate([-sine[:HALF], cosine[:HALF], -sine[HALF:], cosine[HALF:], none], 0)
-    table = jnp.asarray(np.stack([meet_re, meet_im]), jnp.float32)
+    table = np.stack([meet_re, meet_im])
     return table, x_hat, hats, weights
 
 

time: 60.2 us -> 56.7 us (0.942)
  local copies, waits for them, and re-layouts: 12.1 us -> 8.84 us
    unnamed x19 -> x11, local copies, waits for them, and re-layouts: 7.35 us -> 4.09 us
  transfers between devices with their start and end apart: 2 -> 2, of which waited for: 1 -> 1; matrix products, arithmetic and copies ran while one was open for 5% -> 6% of each run, Pallas kernels for 0% -> 0%
where the time goes in v6:
time: 56.7 us; the launch traced here: 56.2 us
  Pallas kernels  24.2 us (43%)
  local copies, waits for them, and re-layouts  8.84 us (16%)
  matrix products  6.66 us (12%)
  starting transfers between devices  5.59 us (10%)
  waiting for transfers between devices  5.44 us (10%)
  blocking collectives  4.58 us (8%)
  other arithmetic  0.83 us (1%)
    pallas_call x1, Pallas kernels, turned_product(): pl.pallas_call(functools.partial(window_kernel, lax.axis_size('rec')), ou...  24.2 us
    ppermute x2, starting transfers between devices, from_behind(): return lax.ppermute(value, axis, pairs)  5.59 us
    ppermute x2, waiting for transfers between devices, from_behind(): return lax.ppermute(value, axis, pairs)  5.44 us
    all_to_all x1, blocking collectives, body(): lax.all_to_all(turned, 'fft', split_axis=2, concat_axis=3, tiled=True)  4.58 us
    unnamed x11, local copies, waits for them, and re-layouts  4.09 us
    all_to_all x2, local copies, waits for them, and re-layouts, body(): lax.all_to_all(turned, 'fft', split_axis=2, concat_axis=3, tiled=True)  1.42 us
    dot_general x2, matrix products, scores(): in_y = jnp.einsum('dcky,cxkz->dxyz', y_turn, volume, precision=HIGH)  1.37 us
    dot_general x1, matrix products, hats_of(): jnp.dot(coords.T, spread, precision=HIGHEST) + offset[None, :]  1.35 us
  transfers between devices with their start and end apart: 2, of which 1 were waited for; matrix products, arithmetic and copies ran while one was open for 6% of the time, Pallas kernels for 0%

profile of v6, /device:TPU:0, one launch (start us, length us, event | category | flops | bytes accessed | tf_op | source)
XLA Modules:
  0.0 56.2 jit_solution(9832508413074309831)
XLA Ops:
  0.0 4.0 %collective-permute-start = (s32[1]{0:T(128)}, s32[1]{0:T(128)}, u32[]{:S(2)}, u32[]{:S(2)}) collective-permute-start(s32[1]{0:T(128)} %param.10), channel_id=1, source_target_pairs={{0,8},{4,12},{8,0},{12,4},{1,9},{5,13},{9,1},{13,5},{2,10},{6,14},... | collective-permute-start | bytes 20 | tf_op jit(solution)/shard_map/ppermute | solution.py:22
  4.0 0.7 %reshape.94 = f32[64,9]{0,1:T(8,128)S(1)} reshape(f32[64,3,3]{0,2,1:T(4,128)} %param.11) | data formatting | bytes 4608 | tf_op jit(solution)/shard_map/reshape | solution.py:265
  4.8 0.1 maximum_subtract_fusion
  4.8 1.0 %fusion.16.weight_ref = f32[512,128]{1,0:T(8,128)S(1)} fusion(s32[512]{0:T(512)} %param.13, f32[128]{0:T(128)S(1)} %fusion.34, f32[18]{0:T(128)} %bitcast.64), kind=kOutput, calls=%fused_computation.18 | convolution fusion | flops 14167296 | bytes 264776 | tf_op jit(solution)/shard_map/dot_general | solution.py:272
  5.9 0.0 collective-permute-done
  5.9 0.8 %convolution_bitcast_fusion.2 = f32[9]{0:T(128)S(1)} fusion(f32[64,9]{0,1:T(8,128)S(1)} %reshape.94, s32[]{:T(128)} %bitcast.1), kind=kOutput, calls=%fused_computation.16 | convolution fusion | flops 6976 | bytes 2344 | tf_op jit(solution)/shard_map/dot_general | solution.py:265
  6.7 0.1 slice.19
  6.8 0.1 slice.20
  6.8 0.1 copy.17
  6.9 0.1 broadcast_bitcast_fusion
  7.0 1.4 %fusion.12.hat_ref = f32[512,256]{1,0:T(8,128)S(1)} fusion(f32[256]{0:T(256)S(1)} %maximum_subtract_fusion, s32[3,512]{1,0:T(4,128)} %param.12, f32[1,3,2,128]{3,2,1,0:T(2,128)S(1)} %broadcast_bitcast_fusion), kind=kOutput, calls=%fused_computation.9 | convolution fusion | flops 5245952 | bytes 534528 | tf_op jit(solution)/shard_map/dot_general | solution.py:282
  8.4 0.9 %fusion.15.x_ref = f32[64,512]{1,0:T(8,128)S(1)} fusion(f32[64]{0:T(128)S(1)} %iota_subtract_fusion, f32[3]{0:T(128)S(1)} %bitcast.65, s32[3,512]{1,0:T(4,128)} %param.12), kind=kOutput, calls=%fused_computation.15 | convolution fusion | flops 1313792 | bytes 137484 | tf_op jit(solution)/shard_map/dot_general | solution.py:284
  9.3 0.0 copy-start
  9.3 1.7 %copy-done = bf16[10,256,512]{2,1,0:T(8,128)(2,1)S(1)} copy-done((bf16[10,256,512]{2,1,0:T(8,128)(2,1)S(1)}, bf16[10,256,512]{2,1,0:T(8,128)(2,1)}, u32[]{:S(2)}) %copy-start) | copy-done | bytes 2621464
  11.1 0.0 copy-start.1
  11.1 1.2 %copy-done.1 = f32[1,1,2,64,2048]{4,3,2,1,0:T(8,128)S(1)} copy-done((f32[1,1,2,64,2048]{4,3,2,1,0:T(8,128)S(1)}, f32[1,1,2,64,2048]{4,3,2,1,0:T(8,128)}, u32[]{:S(2)}) %copy-start.1) | copy-done | bytes 1048600
  12.3 0.0 copy-start.2
  12.3 0.9 %copy-done.2 = f32[272,128]{1,0:T(8,128)S(1)} copy-done((f32[272,128]{1,0:T(8,128)S(1)}, f32[272,128]{1,0:T(8,128)}, u32[]{:S(2)}) %copy-start.2) | copy-done | bytes 139288
  13.2 24.2 %shard_map.100 = f32[128,2048]{1,0:T(8,128)S(1)} custom-call(f32[2,64,2048]{2,1,0:T(8,128)S(1)} %bitcast.61, bf16[10,256,512]{2,1,0:T(8,128)(2,1)S(1)} %copy-done, f32[272,128]{1,0:T(8,128)S(1)} %copy-done.2, f32[64,512]{1,0:T(8,128)S(1)} %fusion.15.x_ref, f32[512,256]{1,0:T(8,128)S(1)} %fusion.12.hat_ref, f32[512,128]{1,0:T(8,128)S(1)} %fusion.16.weight_ref), custom_call_target="tpu_custom_call" | custom-call | tf_op jit(solution)/shard_map/pallas_call | solution.py:232
  37.4 0.8 %copy.18 = f32[1,2,64,2048]{3,1,0,2:T(2,128)S(1)} copy(f32[1,2,64,2048]{3,2,1,0:T(8,128)S(1)} %bitcast.60) | data formatting | bytes 2097152 | tf_op jit(solution)/shard_map/reshape | solution.py:299
  38.2 4.6 %all_to_all.15 = f32[1,2,64,2048]{3,1,0,2:T(2,128)S(1)} all-to-all(f32[1,2,64,2048]{3,1,0,2:T(2,128)S(1)} %copy.18), channel_id=1, replica_groups=mesh['grp'=2,'rec'=4,'chan'=2,'fft'=2] {'fft'}, dimensions={2} | all-to-all | bytes 2097152 | tf_op jit(solution)/shard_map/all_to_all | solution.py:301
  42.8 0.6 %copy.19 = f32[1,2,64,2048]{3,2,1,0:T(8,128)S(1)} copy(f32[1,2,64,2048]{3,1,0,2:T(2,128)S(1)} %all_to_all.15) | data formatting | bytes 2097152 | tf_op jit(solution)/shard_map/all_to_all | solution.py:301
  43.4 0.0 copy-start.4
  43.4 0.8 %copy.20 = f32[1,2,32,2,2048]{4,3,2,1,0:T(2,128)S(1)} copy(f32[1,2,32,2,2048]{4,2,3,1,0:T(8,128)S(1)} %bitcast.62) | data formatting | bytes 2097152 | tf_op jit(solution)/shard_map/all_to_all | solution.py:301
  44.2 1.2 %reshape.97 = f32[2,32,64,64]{3,2,1,0:T(8,128)S(1)} reshape(f32[1,2,32,2,2048]{4,3,2,1,0:T(2,128)S(1)} %copy.20) | data formatting | bytes 2097152 | tf_op jit(solution)/shard_map/reshape | solution.py:302
  45.4 0.0 copy-done.4
  45.4 0.0 copy-start.3
  45.4 0.7 %fusion.7 = f32[2,32,32,64]{3,2,0,1:T(8,128)S(1)} fusion(f32[2,2,2,64,32]{3,4,2,1,0:T(8,128)S(1)} %copy-done.4, s32[]{:T(128)S(6)} %select_n.20, f32[2,32,64,64]{3,2,1,0:T(8,128)S(1)} %reshape.97), kind=kOutput, calls=%fused_computation.5 | convolution fusion | flops 100663296 | bytes 2686980 | tf_op jit(solution)/shard_map/dcky,cxkz->dxyz/dot_general | solution.py:308
  46.1 0.1 copy-done.3
  46.3 0.6 %convolution_bitcast_fusion = f32[32,32,64]{2,1,0:T(8,128)S(1)} fusion(f32[2,32,32,64]{3,2,0,1:T(8,128)S(1)} %fusion.7, f32[2,64,64,1]{2,1,0,3:T(8,128)S(1)} %copy-done.3), kind=kOutput, calls=%fused_computation.10 | convolution fusion | flops 50331648 | bytes 819200 | tf_op jit(solution)/shard_map/dxyz,dzt->xyt/dot_general | solution.py:309
  46.8 0.2 reshape.99
  47.0 1.6 %collective-permute-start.1 = (f32[1,32,2048]{2,1,0:T(8,128)S(1)}, f32[1,32,2048]{2,1,0:T(8,128)S(1)}, u32[]{:S(2)}, u32[]{:S(2)}) collective-permute-start(f32[1,32,2048]{2,1,0:T(8,128)S(1)} %reshape.99), channel_id=1, source_target_pairs={{0,2},{2,0},{1,3},{3,1},{4,6},{6,4},{5,7},{7,5},{8,10},{10,8},{9,1... | collective-permute-start | bytes 786440 | tf_op jit(solution)/shard_map/ppermute | solution.py:22
  48.6 0.7 %fusion.4 = f32[2,32,32,64]{3,2,0,1:T(8,128)S(1)} fusion(f32[2,2,2,64,32]{3,4,2,1,0:T(8,128)S(1)} %copy-done.4, s32[]{:T(128)S(6)} %select_n.19, f32[2,32,64,64]{3,2,1,0:T(8,128)S(1)} %reshape.97), kind=kOutput, calls=%fused_computation.4 | convolution fusion | flops 100663296 | bytes 2686980 | tf_op jit(solution)/shard_map/dcky,cxkz->dxyz/dot_general | solution.py:308
  49.3 0.6 %convolution_bitcast_fusion.1 = f32[32,32,64]{2,1,0:T(8,128)S(1)} fusion(f32[2,32,32,64]{3,2,0,1:T(8,128)S(1)} %fusion.4, f32[2,64,64,1]{2,1,0,3:T(8,128)S(1)} %copy-done.3), kind=kOutput, calls=%fused_computation.11 | convolution fusion | flops 50331648 | bytes 819200 | tf_op jit(solution)/shard_map/dxyz,dzt->xyt/dot_general | solution.py:309
  49.9 0.2 reshape.98
  50.1 5.4 %collective-permute-done.1 = f32[1,32,2048]{2,1,0:T(8,128)S(1)} collective-permute-done((f32[1,32,2048]{2,1,0:T(8,128)S(1)}, f32[1,32,2048]{2,1,0:T(8,128)S(1)}, u32[]{:S(2)}, u32[]{:S(2)}) %collective-permute-start.1) | collective-permute-done | bytes 262176 | tf_op jit(solution)/shard_map/ppermute | solution.py:22
  55.5 0.7 %add.44 = f32[1,32,2048]{2,1,0:T(8,128)} add(f32[1,32,2048]{2,1,0:T(8,128)S(1)} %reshape.98, f32[1,32,2048]{2,1,0:T(8,128)S(1)} %collective-permute-done.1) | non-fusion elementwise | flops 65536 | bytes 786432 | tf_op jit(solution)/shard_map/add | solution.py:320
  (3 shorter events, 0.0 us)
Async XLA Ops:
  0.0 5.9 %collective-permute-start = (s32[1]{0:T(128)}, s32[1]{0:T(128)}, u32[]{:S(2)}, u32[]{:S(2)}) collective-permute-start(s32[1]{0:T(128)} %param.10), channel_id=1, source_target_pairs={{0,8},{4,12},{8,0},{12,4},{1,9},{5,13},{9,1},{13,5},{2,10},{6,14},... | collective-permute-start | bytes 20 | tf_op jit(solution)/shard_map/ppermute | solution.py:22
  9.3 1.7 %copy-start = (bf16[10,256,512]{2,1,0:T(8,128)(2,1)S(1)}, bf16[10,256,512]{2,1,0:T(8,128)(2,1)}, u32[]{:S(2)}) copy-start(bf16[10,256,512]{2,1,0:T(8,128)(2,1)} %constant.52.clone.yt_ref) | copy-start | bytes 7864324
  11.1 1.2 %copy-start.1 = (f32[1,1,2,64,2048]{4,3,2,1,0:T(8,128)S(1)}, f32[1,1,2,64,2048]{4,3,2,1,0:T(8,128)}, u32[]{:S(2)}) copy-start(f32[1,1,2,64,2048]{4,3,2,1,0:T(8,128)} %param.15) | copy-start | bytes 3145732
  12.3 0.9 %copy-start.2 = (f32[272,128]{1,0:T(8,128)S(1)}, f32[272,128]{1,0:T(8,128)}, u32[]{:S(2)}) copy-start(f32[272,128]{1,0:T(8,128)} %constant.53.clone.ft_ref) | copy-start | bytes 417796
  43.4 2.0 %copy-start.4 = (f32[2,2,2,64,32]{3,4,2,1,0:T(8,128)S(1)}, f32[2,2,2,64,32]{3,4,2,1,0:T(8,128)}, u32[]{:S(2)}) copy-start(f32[2,2,2,64,32]{3,4,2,1,0:T(8,128)} %constant.55.clone) | copy-start | bytes 196612
  45.4 0.8 %copy-start.3 = (f32[2,64,64,1]{2,1,0,3:T(8,128)S(1)}, f32[2,64,64,1]{2,1,0,3:T(8,128)}, u32[]{:S(2)}) copy-start(f32[2,64,64,1]{2,1,0,3:T(8,128)} %constant.59) | copy-start | bytes 98308
  47.0 8.5 %collective-permute-start.1 = (f32[1,32,2048]{2,1,0:T(8,128)S(1)}, f32[1,32,2048]{2,1,0:T(8,128)S(1)}, u32[]{:S(2)}, u32[]{:S(2)}) collective-permute-start(f32[1,32,2048]{2,1,0:T(8,128)S(1)} %reshape.99), channel_id=1, source_target_pairs={{0,2},{2,0},{1,3},{3,1},{4,6},{6,4},{5,7},{7,5},{8,10},{10,8},{9,1... | collective-permute-start | bytes 786440 | tf_op jit(solution)/shard_map/ppermute | solution.py:22
